TPU v7x, 32 devices: a whole 2x2x4 slice. The times are simulated.
32 devices in a mesh: dp: 8 (over z, y), mp: 4 (over x, core).
Axes of the slice: x: 2, y: 2, z: 4, core: 2. Of those that a mesh axis runs over, the one named last changes fastest.
Arguments:
- tokens_in: bfloat16 [256, 196, 768], P('dp', None, 'mp'), may hold values from -60 to 60
- cotangent: bfloat16 [256, 196, 768], P(('dp', 'mp')), may hold values from -6 to 6
- ln1_gain: float32 [768], replicated, may hold values from 0.1 to 1.9
- ln1_bias: float32 [768], replicated, may hold values from -3 to 3
- tok_w1: bfloat16 [196, 384], replicated, may hold values from -0.4375 to 0.4375
- tok_b1: float32 [384], replicated, may hold values from -3 to 3
- tok_w2: bfloat16 [384, 196], replicated, may hold values from -0.3125 to 0.3125
- tok_b2: float32 [196], replicated, may hold values from -3 to 3
- second_norm_gain: float32 [768], replicated, may hold values from 0.1 to 1.9
- second_norm_bias: float32 [768], replicated, may hold values from -3 to 3
- chan_w1: bfloat16 [768, 3072], replicated, may hold values from -0.21875 to 0.21875
- chan_b1: float32 [3072], replicated, may hold values from -3 to 3
- chan_w2: bfloat16 [3072, 768], replicated, may hold values from -0.109375 to 0.109375
- chan_b2: float32 [768], replicated, may hold values from -3 to 3
Outputs:
- output: bfloat16 [256, 196, 768], P(('dp', 'mp'))
- tokens_grad: bfloat16 [256, 196, 768], P('dp', None, 'mp')
- ln1_gain_grad: float32 [768], replicated
- ln1_bias_grad: float32 [768], replicated
- tok_w1_grad: float32 [196, 384], replicated
- tok_b1_grad: float32 [384], replicated
- tok_w2_grad: float32 [384, 196], replicated
- tok_b2_grad: float32 [196], replicated
- ln2_gain_grad: float32 [768], replicated
- ln2_bias_grad: float32 [768], replicated
- chan_w1_grad: float32 [768, 3072], replicated
- chan_b1_grad: float32 [3072], replicated
- chan_w2_grad: float32 [3072, 768], replicated
- chan_b2_grad: float32 [768], replicated
All inputs are finite; a program needn't handle non-finite values.
Results may differ from a plain program's by a relative error of at most 0.0076.
Values may be sent and summed in bfloat16 or wider, within the bound.
A program may use at most 256 MiB of HBM per device.

v0:
```python
import jax
import jax.numpy as jnp
from jax import lax
from jax.sharding import PartitionSpec as P

MICRO = 4


EPS = 1e-06


def gelu_value(v):
    return 0.5 * v * (1.0 + lax.erf(v * 0.7071067811865476))


def gelu_slope(v):
    return (
        0.5 * (1.0 + lax.erf(v * 0.7071067811865476))
        + v * jnp.exp(-0.5 * v * v) * 0.3989422804014327
    )


def token_forward(
    value_entries,
    mean_value,
    inverse_deviation,
    gain_vector,
    bias_vector,
    tok_w1,
    tok_b1,
    tok_w2,
    tok_b2,
):
    standardized_input = (value_entries - mean_value[..., None]) * inverse_deviation[..., None]
    normalized_input = (standardized_input * gain_vector + bias_vector).astype(jnp.bfloat16)
    token_preactivation = (
        jnp.einsum("bsc,sh->bhc", normalized_input, tok_w1, preferred_element_type=jnp.float32)
        + tok_b1[None, :, None]
    )
    token_activation = gelu_value(token_preactivation).astype(jnp.bfloat16)
    mixed_output = (
        jnp.einsum("bhc,hs->bsc", token_activation, tok_w2, preferred_element_type=jnp.float32)
        + tok_b2[None, :, None]
    )
    return (
        (value_entries + mixed_output).astype(jnp.bfloat16),
        (standardized_input, normalized_input, token_preactivation, token_activation),
    )


def token_backward_pass(middle_gradient, saved_residuals, gain_vector, tok_w1, tok_w2):
    standardized_input, normalized_input, token_preactivation, token_activation = saved_residuals
    middle_gradient_float = middle_gradient.astype(jnp.float32)
    d_act = jnp.einsum("bsc,hs->bhc", middle_gradient, tok_w2, preferred_element_type=jnp.float32)
    second_weight_gradient = jnp.einsum(
        "bhc,bsc->hs", token_activation, middle_gradient, preferred_element_type=jnp.float32
    )
    second_bias_gradient = jnp.sum(middle_gradient_float, axis=(0, 2))
    d_pre = (d_act * gelu_slope(token_preactivation)).astype(jnp.bfloat16)
    first_weight_gradient = jnp.einsum(
        "bsc,bhc->sh", normalized_input, d_pre, preferred_element_type=jnp.float32
    )
    first_bias_gradient = jnp.sum(d_pre.astype(jnp.float32), axis=(0, 2))
    norm_gradient = jnp.einsum("bhc,sh->bsc", d_pre, tok_w1, preferred_element_type=jnp.float32)
    gain_gradient = jnp.sum(norm_gradient * standardized_input, axis=(0, 1))
    bias_gradient = jnp.sum(norm_gradient, axis=(0, 1))
    standardized_gradient = norm_gradient * gain_vector
    return (
        middle_gradient_float,
        standardized_gradient,
        (first_weight_gradient, first_bias_gradient, second_weight_gradient, second_bias_gradient),
        gain_gradient,
        bias_gradient,
    )


def channel_pass(
    rows, upstream, second_norm_gain, second_norm_bias, chan_w1, chan_b1, chan_w2, chan_b2
):
    count, patches, feature_width = rows.shape
    value_entries = rows.astype(jnp.float32).reshape(count * patches, feature_width)
    mean_value = jnp.sum(value_entries, axis=-1, keepdims=True) / feature_width
    inverse_deviation = lax.rsqrt(
        jnp.sum(value_entries * value_entries, axis=-1, keepdims=True) / feature_width
        - mean_value * mean_value
        + EPS
    )
    standardized_input = (value_entries - mean_value) * inverse_deviation
    normalized_input = (standardized_input * second_norm_gain + second_norm_bias).astype(
        jnp.bfloat16
    )
    pre_chan = jnp.dot(normalized_input, chan_w1, preferred_element_type=jnp.float32) + chan_b1
    act_chan = gelu_value(pre_chan).astype(jnp.bfloat16)
    result = (
        value_entries + jnp.dot(act_chan, chan_w2, preferred_element_type=jnp.float32) + chan_b2
    )
    upstream_rows = upstream.reshape(count * patches, feature_width)
    upstream_float = upstream_rows.astype(jnp.float32)
    grad_w2t = jnp.einsum("rc,rh->ch", upstream_rows, act_chan, preferred_element_type=jnp.float32)
    second_bias_gradient = jnp.sum(upstream_float, axis=0)
    d_act = jnp.einsum("rc,hc->rh", upstream_rows, chan_w2, preferred_element_type=jnp.float32)
    d_pre = (d_act * gelu_slope(pre_chan)).astype(jnp.bfloat16)
    first_weight_gradient = jnp.einsum(
        "rc,rh->ch", normalized_input, d_pre, preferred_element_type=jnp.float32
    )
    first_bias_gradient = jnp.sum(d_pre.astype(jnp.float32), axis=0)
    norm_gradient = jnp.einsum("rh,ch->rc", d_pre, chan_w1, preferred_element_type=jnp.float32)
    gain_gradient = jnp.sum(norm_gradient * standardized_input, axis=0)
    bias_gradient = jnp.sum(norm_gradient, axis=0)
    standardized_gradient = norm_gradient * second_norm_gain
    first_layer = jnp.sum(standardized_gradient, axis=-1, keepdims=True) / feature_width
    second_layer = (
        jnp.sum(standardized_gradient * standardized_input, axis=-1, keepdims=True) / feature_width
    )
    middle_gradient = upstream_float + inverse_deviation * (
        standardized_gradient - first_layer - standardized_input * second_layer
    )
    output = result.astype(jnp.bfloat16).reshape(count, patches, feature_width)
    middle_gradient = middle_gradient.astype(jnp.bfloat16).reshape(count, patches, feature_width)
    return (
        output,
        middle_gradient,
        (
            gain_gradient,
            bias_gradient,
            first_weight_gradient,
            first_bias_gradient,
            grad_w2t,
            second_bias_gradient,
        ),
    )


def body(
    tokens_in,
    cotangent,
    ln1_gain,
    ln1_bias,
    tok_w1,
    tok_b1,
    tok_w2,
    tok_b2,
    second_norm_gain,
    second_norm_bias,
    chan_w1,
    chan_b1,
    chan_w2,
    chan_b2,
):
    groups = lax.axis_size("mp")
    member = lax.axis_index("mp")
    images, patches, local_width = tokens_in.shape
    entire_width = cotangent.shape[2]
    per = cotangent.shape[0] // MICRO
    grouped = tokens_in.reshape(groups, MICRO, per, patches, local_width)
    start = member * local_width
    gain_local = lax.dynamic_slice_in_dim(ln1_gain, start, local_width)
    bias_local = lax.dynamic_slice_in_dim(ln1_bias, start, local_width)
    acc_tok = (
        jnp.zeros(tok_w1.shape, jnp.float32),
        jnp.zeros(tok_b1.shape, jnp.float32),
        jnp.zeros(tok_w2.shape, jnp.float32),
        jnp.zeros(tok_b2.shape, jnp.float32),
    )
    acc_ln1 = (jnp.zeros((entire_width,), jnp.float32), jnp.zeros((entire_width,), jnp.float32))
    acc_chan = (
        jnp.zeros((entire_width,), jnp.float32),
        jnp.zeros((entire_width,), jnp.float32),
        jnp.zeros(chan_w1.shape, jnp.float32),
        jnp.zeros(chan_b1.shape, jnp.float32),
        jnp.zeros(chan_w1.shape, jnp.float32),
        jnp.zeros((entire_width,), jnp.float32),
    )
    outputs = []
    grads_in = []
    for micro in range(MICRO):
        block = grouped[:, micro].reshape(groups * per, patches, local_width)
        upstream = cotangent[micro * per : (micro + 1) * per]
        value_entries = block.astype(jnp.float32)
        sums = lax.psum(
            (jnp.sum(value_entries, axis=-1), jnp.sum(value_entries * value_entries, axis=-1)), "mp"
        )
        mean_value = sums[0] / entire_width
        inverse_deviation = lax.rsqrt(sums[1] / entire_width - mean_value * mean_value + EPS)
        mid, saved_residuals = token_forward(
            value_entries,
            mean_value,
            inverse_deviation,
            gain_local,
            bias_local,
            tok_w1,
            tok_b1,
            tok_w2,
            tok_b2,
        )
        rows = lax.all_to_all(mid, "mp", split_axis=0, concat_axis=2, tiled=True)
        output, middle_gradient, chan_grads = channel_pass(
            rows, upstream, second_norm_gain, second_norm_bias, chan_w1, chan_b1, chan_w2, chan_b2
        )
        d_cols = lax.all_to_all(middle_gradient, "mp", split_axis=2, concat_axis=0, tiled=True)
        (
            middle_gradient_float,
            standardized_gradient,
            token_gradients,
            gain_gradient,
            bias_gradient,
        ) = token_backward_pass(d_cols, saved_residuals, gain_local, tok_w1, tok_w2)
        standardized_input = saved_residuals[0]
        backward_result = lax.psum(
            (
                jnp.sum(standardized_gradient, axis=-1),
                jnp.sum(standardized_gradient * standardized_input, axis=-1),
            ),
            "mp",
        )
        d_input = middle_gradient_float + inverse_deviation[..., None] * (
            standardized_gradient
            - backward_result[0][..., None] / entire_width
            - standardized_input * backward_result[1][..., None] / entire_width
        )
        d_input = d_input.astype(jnp.bfloat16)
        gain_gradient = lax.dynamic_update_slice_in_dim(
            jnp.zeros((entire_width,), jnp.float32), gain_gradient, start, 0
        )
        bias_gradient = lax.dynamic_update_slice_in_dim(
            jnp.zeros((entire_width,), jnp.float32), bias_gradient, start, 0
        )
        outputs.append(output)
        grads_in.append(d_input.reshape(groups, per, patches, local_width))
        acc_tok = tuple((a + b for a, b in zip(acc_tok, token_gradients)))
        acc_ln1 = (acc_ln1[0] + gain_gradient, acc_ln1[1] + bias_gradient)
        acc_chan = tuple((a + b for a, b in zip(acc_chan, chan_grads)))
    output_all = jnp.concatenate(outputs, axis=0)
    tokens_grad = jnp.stack(grads_in, axis=1).reshape(images, patches, local_width)
    summed = lax.psum(
        (
            acc_ln1[0],
            acc_ln1[1],
            acc_tok[0],
            acc_tok[1],
            acc_tok[2],
            acc_tok[3],
            acc_chan[0],
            acc_chan[1],
            acc_chan[2],
            acc_chan[3],
            acc_chan[4],
            acc_chan[5],
        ),
        ("dp", "mp"),
    )
    g_ln1, b_ln1, g_tw1, g_tb1, g_tw2, g_tb2, g_ln2, b_ln2, g_cw1, g_cb1, g_cw2t, g_cb2 = summed
    return (
        output_all,
        tokens_grad,
        g_ln1,
        b_ln1,
        g_tw1,
        g_tb1,
        g_tw2,
        g_tb2,
        g_ln2,
        b_ln2,
        g_cw1,
        g_cb1,
        g_cw2t.T,
        g_cb2,
    )


def solution(mesh):
    placed = (
        P("dp", None, "mp"),
        P(("dp", "mp"), None, None),
        P(),
        P(),
        P(),
        P(),
        P(),
        P(),
        P(),
        P(),
        P(),
        P(),
        P(),
        P(),
    )
    return jax.shard_map(
        body,
        mesh=mesh,
        in_specs=placed,
        out_specs=(
            P(("dp", "mp"), None, None),
            P("dp", None, "mp"),
            P(),
            P(),
            P(),
            P(),
            P(),
            P(),
            P(),
            P(),
            P(),
            P(),
            P(),
            P(),
        ),
        check_vma=False,
    )
```

profile of v0, /device:TPU:0, one launch (start us, length us, event | category | flops | bytes accessed | tf_op | source)
XLA Modules:
  0.0 660.3 jit_solution(11049145741682172729)
XLA Ops:
  7.2 3.3 convert_reduce_fusion.15
  13.8 13.5 %all-reduce.3 = (f32[8,196]{1,0:T(8,128)S(1)}, f32[8,196]{1,0:T(8,128)S(1)}, f32[8,196]{1,0:T(8,128)S(1)}, f32[8,196]{1,0:T(8,128)S(1)}, f32[8,196]{1,0:T(8,128)...) all-reduce(f32[8,196]{1,0:T(8,128)S(1)} %reduce_sum.613, ...), channel_id=1, replica_groups=mesh['dp'=8,'mp'=4] {'mp'}, use_global_device_ids=true, to_apply=%region_21.0 | all-reduce | flops 12544 | bytes 100352 | tf_op jit(solution)/shard_map/psum | solution.py:180
  27.4 3.2 bitcast_subtract_fusion
  33.9 5.1 fusion.61
  41.4 3.5 all-to-all-start
  44.9 2.4 convert_reduce_fusion.18
  47.3 2.7 fusion.125
  55.3 2.8 fusion.68
  61.6 3.7 all-to-all-start.1
  68.0 8.9 %all-to-all-done.1 = bf16[8,196,192]{1,2,0:T(8,128)(2,1)S(1)} async-done(((bf16[8,196,192]{1,2,0:T(8,128)(2,1)}), bf16[8,196,192]{1,2,0:T(8,128)(2,1)S(1)}, u32[]{:S(2)}, u32[]{:S(2)}) %all-to-all-start.1) | async-done | bytes 602144 | tf_op jit(solution)/shard_map/all_to_all | solution.py:196
  76.9 4.2 all-to-all-start.2
  87.0 5.0 fusion.121
  92.0 7.5 %convert_reduce_fusion.2 = (f32[3072]{0:T(1024)}, bf16[392,3072]{1,0:T(8,128)(2,1)S(1)}) fusion(f32[392,3072]{1,0:T(8,128)S(1)} %fusion.121, f32[3072]{0:T(1024)S(1)} %copy-done.101, bf16[392,768]{1,0:T(8,128)(2,1)S(1)} %copy-done.57, bf16[3072,768]{1,0:T(8,128)(2,1)} %param.26), kind=kOutput, calls=%fused_computation.32 | convolution fusion | flops 1865339904 | bytes 12570624 | tf_op jit(solution)/shard_map/rc,hc->rh/dot_general | solution.py:101
  99.5 3.1 fusion.130
  102.7 5.3 fusion.120
  108.0 4.6 all-to-all-start.3
  119.4 5.3 fusion.123
  124.8 10.7 %multiply_convert_fusion.3 = (bf16[392,3072]{1,0:T(8,128)(2,1)}, bf16[392,3072]{1,0:T(8,128)(2,1)}, bf16[392,3072]{1,0:T(8,128)(2,1)}, f32[392,3072]{1,0:T(8,128)S(1)}) fusion(f32[3072]{0:T(1024)S(1)} %copy-done.101, f32[392,3072]{1,0:T(8,128)S(1)} %fusion.123, f32[392,3072]{1,0:T(8,128)} %copy-done.114, bf16[768,3072]{1,0:T(8,128)(2,1)} %param.24, ...), kind=kOutput, calls=%fused_computation.40 | convolution fusion | flops 1872869376 | bytes 27620416 | tf_op jit(solution)/shard_map/dot_general | solution.py:92
  135.5 3.5 convert_reduce_fusion.3
  139.1 3.1 fusion.129
  142.2 5.3 fusion.118
  152.4 6.1 convert_reduce_fusion.1
  158.6 6.3 fusion.122
  164.9 6.2 multiply_reduce_fusion.9
  171.3 2.2 fusion.124
  173.6 3.6 convert_reduce_fusion
  177.2 3.9 multiply_reduce_fusion.8
  183.2 3.0 copy.80
  186.2 4.4 all-to-all-start.6
  190.6 8.3 %fusion.132 = f32[3072,768]{1,0:T(8,128)} fusion(bf16[392,3072]{1,0:T(8,128)(2,1)} %get-tuple-element.142, bf16[392,768]{1,0:T(8,128)(2,1)} %reshape.329), kind=kOutput, calls=%fused_computation.304 | convolution fusion | flops 1849688064 | bytes 12447744 | tf_op jit(solution)/shard_map/rc,rh->ch/dot_general | solution.py:99
  198.9 6.1 fusion.133
  205.1 5.2 fusion.131
  211.6 15.2 %add_add_fusion.1 = f32[768,3072]{1,0:T(8,128)} fusion(f32[768,3072]{1,0:T(8,128)} %fusion.122, f32[768,3072]{1,0:T(8,128)} %fusion.118, f32[768,3072]{1,0:T(8,128)S(1)} %bitcast.431, bf16[392,3072]{1,0:T(8,128)(2,1)} %copy-done.56, f32[392,768]{1,0:T(8,128)S(1)} %reshape.343, f32[392]{0:T(512)S(1)} %add_rsqrt_fusion.4, f32[392]{0:T(512)S(1)} %div.133, ...), kind=kOutput, calls=%fused_computation.1 | convolution fusion | flops 1858271232 | bytes 41370688 | tf_op jit(solution)/shard_map/rc,rh->ch/dot_general | solution.py:103
  226.8 16.0 %add_add_fusion = f32[3072,768]{1,0:T(8,128)} fusion(f32[3072,768]{1,0:T(8,128)} %fusion.133, f32[3072,768]{1,0:T(8,128)} %fusion.131, f32[3072,768]{1,0:T(8,128)} %fusion.132, bf16[392,768]{1,0:T(8,128)(2,1)S(1)} %copy-done.35, f32[392,3072]{1,0:T(8,128)} %copy-done.36, f32[3072]{0:T(1024)S(1)} %copy-done.101), kind=kOutput, calls=%fused_computation | convolution fusion | flops 1863991296 | bytes 43180032 | tf_op jit(solution)/shard_map/rc,rh->ch/dot_general | solution.py:99
  244.9 3.0 copy.72
  247.9 3.2 add_convert_fusion.10
  254.3 2.2 copy.84
  256.5 4.2 all-to-all-start.7
  260.7 3.0 copy.91
  266.6 3.5 convert_reduce_fusion.5
  270.1 2.4 all-to-all-done.7
  272.5 4.2 all-to-all-start.5
  276.7 3.0 copy.92
  280.4 2.8 convolution_bitcast_fusion
  283.2 3.4 convert_reduce_fusion.4
  288.4 4.2 all-to-all-start.4
  292.6 3.0 copy.90
  296.3 2.8 convolution_bitcast_fusion.2
  299.1 3.5 convert_reduce_fusion.6
  304.3 3.1 copy.89
  307.4 3.1 convolution_bitcast_fusion.5
  314.0 3.1 convert_reduce_fusion.7
  321.0 7.2 %fusion.84 = bf16[392,768]{1,0:T(8,128)(2,1)} fusion(f32[392,768]{1,0:T(8,128)S(1)} %reshape.343, bf16[3072,768]{1,0:T(8,128)(2,1)} %param.26, f32[768]{0:T(1024)S(1)} %copy-done.112, f32[392,3072]{1,0:T(8,128)} %copy-done.36, f32[3072]{0:T(1024)S(1)} %copy-done.101), kind=kOutput, calls=%fused_computation.168 | convolution fusion | flops 1857816576 | bytes 11357184 | tf_op jit(solution)/shard_map/dot_general | solution.py:95
  329.4 5.1 fusion.87
  334.7 6.5 fusion.85
  343.2 6.1 fusion.86
  360.6 4.3 multiply_reduce_fusion.7
  366.6 12.0 %all-reduce.2 = (f32[8,196]{1,0:T(8,128)S(1)}, f32[8,196]{1,0:T(8,128)S(1)}, f32[8,196]{1,0:T(8,128)S(1)}, f32[8,196]{1,0:T(8,128)S(1)}, f32[8,196]{1,0:T(8,128)...) all-reduce(f32[8,196]{1,0:T(8,128)S(1)} %get-tuple-element.45, ...), channel_id=1, replica_groups=mesh['dp'=8,'mp'=4] {'mp'}, use_global_device_ids=true, to_apply=%region_47.0 | all-reduce | flops 12544 | bytes 100352 | tf_op jit(solution)/shard_map/psum | solution.py:209
  378.7 4.1 add_convert_fusion.1
  382.8 3.3 bitcast_subtract_fusion.3
  398.5 42.3 %all-reduce = (f32[768]{0:T(1024)}, f32[768]{0:T(1024)}, f32[384]{0:T(512)}, f32[196]{0:T(256)}, f32[768]{0:T(1024)}, /*index=5*/f32[768]{0:T(1024)}, f32[3072]{0:T(1024)}, f32[768]{0:T(1024)}) all-reduce(f32[768]{0:T(1024)S(1)} %add_dynamic-update-slice_fusion.3, ...), channel_id=1, replica_groups=mesh['dp'=8,'mp'=4] {'dp','mp'}, use_global_device_ids=true, to_apply=%region_52.0 | all-reduce | flops 7492 | bytes 59936 | tf_op jit(solution)/shard_map/psum | solution.py:235
  440.8 196.4 %all-reduce.6.cloned.1.call-done = (f32[196,384]{1,0:T(8,128)}, f32[384,196]{0,1:T(8,128)}, f32[768,3072]{1,0:T(8,128)}, f32[3072,768]{1,0:T(8,128)}) async-done(((f32[196,384]{1,0:T(8,128)}, f32[384,196]{0,1:T(8,128)}, f32[768,3072]{1,0:T(8,128)}, f32[3072,768]{1,0:T(8,128)}), (f32[196,384]{1,0:T(8,128)}, f32[384,196]{0,1:T(8,128)}, f32[768,3072]{1,0:T(8,128)}, ...) | async-done | bytes 19476496 | tf_op jit(solution)/shard_map/psum | solution.py:235
  640.7 8.8 %copy.112 = f32[768,3072]{1,0:T(8,128)} copy(f32[768,3072]{1,0:T(8,128)} %get-tuple-element.207) | data formatting | bytes 18874368
  649.5 3.7 copy.113
  (405 shorter events, 93.4 us)
Async XLA Ops:
  7.2 23.6 %copy-start = (bf16[196,384]{1,0:T(8,128)(2,1)S(1)}, bf16[196,384]{1,0:T(8,128)(2,1)}, u32[]{:S(2)}) copy-start(bf16[196,384]{1,0:T(8,128)(2,1)} %param.18) | copy-start | bytes 451588
  13.0 17.7 %copy-start.99 = (f32[192]{0:T(256)}, f32[192]{0:T(256)S(1)}, u32[]{:S(2)}) copy-start(f32[192]{0:T(256)S(1)} %dynamic_slice.6) | copy-start | bytes 2308
  33.0 5.9 copy-start.9
  33.8 6.1 copy-start.78
  33.8 6.1 copy-start.108
  33.8 6.1 copy-start.113
  39.9 5.0 copy-start.8
  41.4 20.2 %all-to-all-start = ((bf16[8,196,192]{1,2,0:T(8,128)(2,1)}), bf16[8,196,192]{1,2,0:T(8,128)(2,1)S(1)}, u32[]{:S(2)}, u32[]{:S(2)}) async-start(bf16[8,196,192]{1,2,0:T(8,128)(2,1)} %fusion.74), calls=%async_computation | async-start | bytes 1572864 | tf_op jit(solution)/shard_map/all_to_all | solution.py:196
  61.6 15.3 %all-to-all-start.1 = ((bf16[8,196,192]{1,2,0:T(8,128)(2,1)}), bf16[8,196,192]{1,2,0:T(8,128)(2,1)S(1)}, u32[]{:S(2)}, u32[]{:S(2)}) async-start(bf16[8,196,192]{1,2,0:T(8,128)(2,1)} %fusion.72), calls=%async_computation.1 | async-start | bytes 1572864 | tf_op jit(solution)/shard_map/all_to_all | solution.py:196
  76.9 4.2 copy-start.54
  76.9 31.1 %all-to-all-start.2 = ((bf16[8,196,192]{1,2,0:T(8,128)(2,1)}), bf16[8,196,192]{1,2,0:T(8,128)(2,1)}, u32[]{:S(2)}, u32[]{:S(2)}) async-start(bf16[8,196,192]{1,2,0:T(8,128)(2,1)} %fusion.70), calls=%async_computation.2 | async-start | bytes 1572864 | tf_op jit(solution)/shard_map/all_to_all | solution.py:196
  86.9 5.1 copy-start.57
  86.9 5.1 copy-start.101
  86.9 12.6 %slice-start.6 = ((s8[4718592]{0:T(1024)(128)(4,1)}), s8[4194304]{0:T(1024)(128)(4,1)S(1)}, s32[]{:S(2)}) async-start(s8[4718592]{0:T(1024)(128)(4,1)} %bitcast.453), calls=%async_computation.15 | async-start | bytes 8388608
  92.0 7.5 %copy-start.114 = (f32[392,3072]{1,0:T(8,128)}, f32[392,3072]{1,0:T(8,128)S(1)}, u32[]{:S(2)}) copy-start(f32[392,3072]{1,0:T(8,128)S(1)} %fusion.121) | copy-start | bytes 14450692
  92.0 7.5 %slice-start.7 = ((s8[4718592]{0:T(1024)(128)(4,1)}), s8[524288]{0:T(1024)(128)(4,1)S(1)}, s32[]{:S(2)}) async-start(s8[4718592]{0:T(1024)(128)(4,1)} %bitcast.453), calls=%async_computation.16 | async-start | bytes 1048576
  108.0 39.6 %all-to-all-start.3 = ((bf16[8,196,192]{1,2,0:T(8,128)(2,1)}), bf16[8,196,192]{1,2,0:T(8,128)(2,1)}, u32[]{:S(2)}, u32[]{:S(2)}) async-start(bf16[8,196,192]{1,2,0:T(8,128)(2,1)} %fusion.68), calls=%async_computation.3 | async-start | bytes 1572864 | tf_op jit(solution)/shard_map/all_to_all | solution.py:196
  119.3 22.9 %copy-start.40 = (f32[392,768]{1,0:T(8,128)}, f32[392,768]{1,0:T(8,128)S(1)}, u32[]{:S(2)}) copy-start(f32[392,768]{1,0:T(8,128)S(1)} %reshape.337) | copy-start | bytes 3612676
  119.4 16.1 %slice-start.12 = ((s8[4718592]{0:T(1024)(128)(4,1)}), s8[4194304]{0:T(1024)(128)(4,1)S(1)}, s32[]{:S(2)}) async-start(s8[4718592]{0:T(1024)(128)(4,1)} %bitcast.459), calls=%async_computation.21 | async-start | bytes 8388608
  119.4 19.7 %slice-start.8 = ((s8[4718592]{0:T(1024)(128)(4,1)}), s8[4194304]{0:T(1024)(128)(4,1)S(1)}, s32[]{:S(2)}) async-start(s8[4718592]{0:T(1024)(128)(4,1)} %bitcast.455), calls=%async_computation.17 | async-start | bytes 8388608
  124.7 10.8 %copy-start.115 = (f32[392,3072]{1,0:T(8,128)}, f32[392,3072]{1,0:T(8,128)S(1)}, u32[]{:S(2)}) copy-start(f32[392,3072]{1,0:T(8,128)S(1)} %fusion.123) | copy-start | bytes 14450692
  124.7 10.7 %copy-start.58 = (bf16[392,768]{1,0:T(8,128)(2,1)S(1)}, bf16[392,768]{1,0:T(8,128)(2,1)}, u32[]{:S(2)}) copy-start(bf16[392,768]{1,0:T(8,128)(2,1)} %reshape.327) | copy-start | bytes 1806340
  124.7 10.7 %slice-start.13 = ((s8[4718592]{0:T(1024)(128)(4,1)}), s8[524288]{0:T(1024)(128)(4,1)S(1)}, s32[]{:S(2)}) async-start(s8[4718592]{0:T(1024)(128)(4,1)} %bitcast.459), calls=%async_computation.22 | async-start | bytes 1048576
  124.8 14.3 %slice-start.9 = ((s8[4718592]{0:T(1024)(128)(4,1)}), s8[524288]{0:T(1024)(128)(4,1)S(1)}, s32[]{:S(2)}) async-start(s8[4718592]{0:T(1024)(128)(4,1)} %bitcast.455), calls=%async_computation.18 | async-start | bytes 1048576
  152.4 6.1 copy-start.70
  158.5 6.3 copy-start.38
  158.5 6.3 copy-start.41
  158.5 6.3 copy-start.71
  158.6 6.3 copy-start.72
  158.6 12.7 %slice-start.10 = ((s8[4718592]{0:T(1024)(128)(4,1)}), s8[4194304]{0:T(1024)(128)(4,1)S(1)}, s32[]{:S(2)}) async-start(s8[4718592]{0:T(1024)(128)(4,1)} %bitcast.457), calls=%async_computation.19 | async-start | bytes 8388608
  158.6 14.9 %slice-start.14 = ((s8[4718592]{0:T(1024)(128)(4,1)}), s8[4194304]{0:T(1024)(128)(4,1)S(1)}, s32[]{:S(2)}) async-start(s8[4718592]{0:T(1024)(128)(4,1)} %bitcast.461), calls=%async_computation.23 | async-start | bytes 8388608
  164.9 6.4 slice-start.11
  164.9 8.6 %slice-start.15 = ((s8[4718592]{0:T(1024)(128)(4,1)}), s8[524288]{0:T(1024)(128)(4,1)S(1)}, s32[]{:S(2)}) async-start(s8[4718592]{0:T(1024)(128)(4,1)} %bitcast.461), calls=%async_computation.24 | async-start | bytes 1048576
  186.2 70.3 %all-to-all-start.6 = ((bf16[2,196,768]{1,0,2:T(2,128)(2,1)}), bf16[2,196,768]{1,0,2:T(2,128)(2,1)}, u32[]{:S(2)}, u32[]{:S(2)}) async-start(bf16[2,196,768]{1,0,2:T(2,128)(2,1)} %copy.80), calls=%async_computation.6 | async-start | bytes 1572864 | tf_op jit(solution)/shard_map/all_to_all | solution.py:200
  190.6 8.3 %copy-start.80 = (bf16[392,768]{1,0:T(8,128)(2,1)S(1)}, bf16[392,768]{1,0:T(8,128)(2,1)}, u32[]{:S(2)}) copy-start(bf16[392,768]{1,0:T(8,128)(2,1)} %reshape.331) | copy-start | bytes 1806340
  190.6 8.3 %copy-start.116 = (bf16[392,3072]{1,0:T(8,128)(2,1)S(1)}, bf16[392,3072]{1,0:T(8,128)(2,1)}, u32[]{:S(2)}) copy-start(bf16[392,3072]{1,0:T(8,128)(2,1)} %get-tuple-element.141) | copy-start | bytes 7225348
  198.9 6.2 copy-start.59
  198.9 6.2 copy-start.117
  198.9 12.7 %slice-start = ((s8[9437184]{0:T(1024)(128)(4,1)}), s8[4194304]{0:T(1024)(128)(4,1)S(1)}, s32[]{:S(2)}) async-start(s8[9437184]{0:T(1024)(128)(4,1)} %bitcast.430), calls=%async_computation.9 | async-start | bytes 8388608
  198.9 12.6 %slice-start.1 = ((s8[9437184]{0:T(1024)(128)(4,1)}), s8[4194304]{0:T(1024)(128)(4,1)S(1)}, s32[]{:S(2)}) async-start(s8[9437184]{0:T(1024)(128)(4,1)} %bitcast.430), calls=%async_computation.10 | async-start | bytes 8388608
  205.1 5.2 copy-start.42
  205.1 5.2 copy-start.73
  205.1 6.5 slice-start.2
  256.5 15.9 %all-to-all-start.7 = ((bf16[2,196,768]{1,0,2:T(2,128)(2,1)}), bf16[2,196,768]{1,0,2:T(2,128)(2,1)}, u32[]{:S(2)}, u32[]{:S(2)}) async-start(bf16[2,196,768]{1,0,2:T(2,128)(2,1)} %copy.84), calls=%async_computation.7 | async-start | bytes 1572864 | tf_op jit(solution)/shard_map/all_to_all | solution.py:200
  264.4 5.6 copy-start.22
  272.5 15.9 %all-to-all-start.5 = ((bf16[2,196,768]{1,0,2:T(2,128)(2,1)}), bf16[2,196,768]{1,0,2:T(2,128)(2,1)}, u32[]{:S(2)}, u32[]{:S(2)}) async-start(bf16[2,196,768]{1,0,2:T(2,128)(2,1)} %copy.76), calls=%async_computation.5 | async-start | bytes 1572864 | tf_op jit(solution)/shard_map/all_to_all | solution.py:200
  280.3 6.3 copy-start.23
  288.4 15.9 %all-to-all-start.4 = ((bf16[2,196,768]{1,0,2:T(2,128)(2,1)}), bf16[2,196,768]{1,0,2:T(2,128)(2,1)}, u32[]{:S(2)}, u32[]{:S(2)}) async-start(bf16[2,196,768]{1,0,2:T(2,128)(2,1)} %copy.72), calls=%async_computation.4 | async-start | bytes 1572864 | tf_op jit(solution)/shard_map/all_to_all | solution.py:200
  292.6 344.5 %all-reduce.6.cloned.1.call-start = ((), (), s32[]{:S(2)}) async-start(), calls=%async_computation.8 | async-start | bytes 38977536 | tf_op jit(solution)/shard_map/psum | solution.py:235
  296.3 6.3 copy-start.24
  304.3 6.2 copy-start.31
  307.4 5.9 copy-start.18
  321.0 8.4 %copy-start.43 = (f32[392,768]{1,0:T(8,128)S(1)}, f32[392,768]{1,0:T(8,128)}, u32[]{:S(2)}) copy-start(f32[392,768]{1,0:T(8,128)} %copy-done.40) | copy-start | bytes 3612676
  334.7 8.5 %copy-start.39 = (f32[392,768]{1,0:T(8,128)S(1)}, f32[392,768]{1,0:T(8,128)}, u32[]{:S(2)}) copy-start(f32[392,768]{1,0:T(8,128)} %reshape.339) | copy-start | bytes 3612676
  352.8 5.9 copy-start.75
  357.9 7.1 %copy-start.33 = (f32[8,192,196]{2,1,0:T(8,128)}, f32[8,192,196]{2,1,0:T(8,128)S(1)}, u32[]{:S(2)}) copy-start(f32[8,192,196]{2,1,0:T(8,128)S(1)} %get-tuple-element.176) | copy-start | bytes 3612676
  358.7 6.3 copy-start.34
  378.6 4.2 copy-start.4
  378.6 4.2 copy-start.6
  378.6 4.2 copy-start.25
  391.3 4.8 copy-start.5
  638.8 10.6 %slice-start.3 = ((s8[9437184]{0:T(1024)(128)(4,1)}), s8[4194304]{0:T(1024)(128)(4,1)S(1)}, s32[]{:S(2)}) async-start(s8[9437184]{0:T(1024)(128)(4,1)} %bitcast.432), calls=%async_computation.12 | async-start | bytes 8388608
  640.7 8.8 %slice-start.4 = ((s8[9437184]{0:T(1024)(128)(4,1)}), s8[4194304]{0:T(1024)(128)(4,1)S(1)}, s32[]{:S(2)}) async-start(s8[9437184]{0:T(1024)(128)(4,1)} %bitcast.432), calls=%async_computation.13 | async-start | bytes 8388608
  640.7 8.8 %slice-start.5 = ((s8[9437184]{0:T(1024)(128)(4,1)}), s8[1048576]{0:T(1024)(128)(4,1)S(1)}, s32[]{:S(2)}) async-start(s8[9437184]{0:T(1024)(128)(4,1)} %bitcast.432), calls=%async_computation.14 | async-start | bytes 2097152
  (79 other events, 198.5 us)
Sparse Core Ops, SparseCore 0:
  320.5 316.5 all-reduce.5
where the time goes:
time: 670 us; the launch traced here: 660 us
  waiting for transfers between devices  211 us (31%)
  matrix products  203 us (30%)
  local copies, waits for them, and re-layouts  87.8 us (13%)
  blocking collectives  67.8 us (10%)
  other arithmetic  41.8 us (6%)
  starting transfers between devices  33 us (5%)
  between operations  16.1 us (2%)
    psum x1, waiting for transfers between devices, body(): lax.psum((acc_ln1[0], acc_ln1[1], acc_tok[0], acc_tok[1], acc_tok[2], acc...  196 us
    psum x1, blocking collectives, body(): lax.psum((acc_ln1[0], acc_ln1[1], acc_tok[0], acc_tok[1], acc_tok[2], acc...  42.3 us
    dot_general x4, matrix products, channel_pass(): jnp.einsum('rc,rh->ch', upstream_rows, act_chan, preferred_element_type=j...  35.6 us
    dot_general x4, matrix products, channel_pass(): jnp.einsum('rc,rh->ch', normalized_input, d_pre, preferred_element_type=j...  32.1 us
    unnamed x274, local copies, waits for them, and re-layouts  27.9 us
    dot_general x4, matrix products, channel_pass(): jnp.dot(act_chan, chan_w2, preferred_element_type=jnp.float32)  24.9 us
    dot_general x4, matrix products, channel_pass(): jnp.dot(normalized_input, chan_w1, preferred_element_type=jnp.float32)  23.3 us
    dot_general x4, matrix products, channel_pass(): jnp.einsum('rc,hc->rh', upstream_rows, chan_w2, preferred_element_type=jn...  20.8 us
  transfers between devices with their start and end apart: 9, of which 5 were waited for; matrix products, arithmetic and copies ran while one was open for 36% of the time, Pallas kernels for 0%

commit v1 on v0

v1 whole, which is shorter than its diff:
```python
import functools

import jax
import jax.numpy as jnp
from jax import lax
from jax.experimental import pallas as pl
from jax.experimental.pallas import tpu as pltpu
from jax.sharding import PartitionSpec as P

BF = jnp.bfloat16
F32 = jnp.float32
EPS = 1e-06
MESH = pl.DeviceIdType.MESH
NT = (((1,), (1,)), ((), ()))

BLOCK = 512
POINTS = 3
SLOTS = 3
SPACE = 256
LAGS = (0, 1, 4, 6, 7, 8, 9, 10, 12, 15, 16)


def dot(a, b):
    return jnp.dot(a, b, preferred_element_type=F32)


def dot_nt(a, b):
    return lax.dot_general(a, b, NT, preferred_element_type=F32)


def gelu_both(v):
    cdf = 0.5 + 0.5 * lax.erf(v * 0.7071067811865476)
    return v * cdf, cdf + v * (jnp.exp(-0.5 * v * v) * 0.3989422804014327)


def standardize(v, axis):
    width = v.shape[axis]
    mean = jnp.sum(v, axis=axis, keepdims=True) / width
    square = jnp.sum(v * v, axis=axis, keepdims=True) / width
    rstd = lax.rsqrt(square - mean * mean + EPS)
    return (v - mean) * rstd, rstd


def bits_of(n):
    return n.bit_length() - 1


def reduce_plan(n_mp, n_dp, width):
    dp = [("dp", b) for b in range(bits_of(n_dp))]
    mp = [("mp", b) for b in range(1, bits_of(n_mp))]
    if len(dp) == 3 and len(mp) == 1:
        cut = width * 2 // 3
        raw = [(0, cut, [dp[0], mp[0], dp[1], dp[2]]), (cut, width - cut, [dp[1], dp[2], dp[0], mp[0]])]
    else:
        raw = [(0, width, dp + mp)]
    streams = []
    for base, rows, keys in raw:
        stages, have = [], rows
        for key in keys:
            halved = have % 32 == 0
            have = have // 2 if halved else have
            stages.append((key, have, halved))
        streams.append((base, rows, stages))
    return streams


def dp_groups(n_dp):
    groups, stride = [], 1
    while stride < n_dp:
        size = min(8, n_dp // stride)
        groups.append((stride, size))
        stride *= size
    return groups


def layer_kernel(
    n_mp,
    n_dp,
    streams,
    groups,
    tokens,
    cot,
    w1,
    w2,
    g1,
    c1,
    tw1,
    tb1,
    tw2,
    tb2,
    g2,
    c2,
    b1,
    b2,
    out_o,
    dtok_o,
    gw_o,
    smt_o,
    smv_o,
    x_in,
    g_in,
    mid_p,
    g_f,
    g_t,
    n2_f,
    n2_t,
    act_t,
    slope_t,
    out_a,
    dn_a,
    act_s,
    dp_s,
    w1_s,
    w2_s,
    part,
    r0,
    rest,
    n1_s,
    dm_s,
    dm_t,
    tw1p,
    tw1t,
    tw2p,
    tw2t,
    rows_s,
    b1_s,
    cols_s,
    cb1_a,
    va,
    ln1_a,
    tg_a,
    t_b,
    t_r1,
    t_s1,
    t_r2,
    t_s2,
    t_g,
    v_b,
    v_r1,
    v_s1,
    v_r2,
    in_s,
    in_r,
    in_l,
    g_l,
    w_l,
    o_l,
    out_s,
    out_r,
    out_l,
    rs_s,
    rs_r,
    ag_s,
    ag_r,
    own_l,
    sm_s,
    sm_r,
    sm_l,
):
    images, width, patches = x_in.shape
    local = tokens.shape[1]
    hidden = tw1.shape[1]
    blocks = w1.shape[1] // BLOCK
    total = images * patches
    half = total // 2
    mp_me = lax.axis_index("mp")
    dp_me = lax.axis_index("dp")

    def bit_of(key):
        axis, b = key
        me = mp_me if axis == "mp" else dp_me
        return (me // (1 << b)) % 2

    def partner(key):
        axis, b = key
        me = mp_me if axis == "mp" else dp_me
        return {axis: me + (1 << b) * (1 - 2 * bit_of(key))}

    def member(group):
        stride, size = group
        return (dp_me // stride) % size

    def peer(group, k):
        stride, size = group
        mine = member(group)
        other = lax.rem(mine + k, size)
        return other, {"dp": dp_me + (other - mine) * stride}

    def mp_peer(k):
        other = lax.rem(mp_me + k, n_mp)
        return other, {"mp": other}

    def remote(src, dst, send, recv, to):
        return pltpu.make_async_remote_copy(
            src_ref=src, dst_ref=dst, send_sem=send, recv_sem=recv, device_id=to, device_id_type=MESH
        )

    barrier = pltpu.get_barrier_semaphore()
    count = 0
    for k in range(1, n_mp):
        pl.semaphore_signal(barrier, inc=1, device_id=mp_peer(k)[1], device_id_type=MESH)
        count += 1
    for group in groups:
        for k in range(1, group[1]):
            pl.semaphore_signal(barrier, inc=1, device_id=peer(group, k)[1], device_id_type=MESH)
            count += 1

    def channels(member):
        return pl.ds(pl.multiple_of(member * local, 16), local)

    def own_tokens(b):
        return pltpu.make_async_copy(tokens.at[mp_me * images + b], x_in.at[b, channels(mp_me)], in_l.at[b])

    own_cot = pltpu.make_async_copy(cot, n2_f, g_l.at[0])

    def weights(j):
        slot = lax.rem(j, 2)
        cols = pl.ds(pl.multiple_of(j * BLOCK, BLOCK), BLOCK)
        return (
            pltpu.make_async_copy(w1.at[:, cols], w1_s.at[slot], w_l.at[0, slot]),
            pltpu.make_async_copy(w2.at[cols], w2_s.at[slot], w_l.at[1, slot]),
        )

    def load_own(b, _):
        own_tokens(b).start()
        return 0

    own_cot.start()
    lax.fori_loop(0, images, load_own, 0)
    for copy in weights(0):
        copy.start()

    pl.semaphore_wait(barrier, count)

    def token_copy(k, b):
        other, to = mp_peer(k)
        return remote(
            tokens.at[other * images + b], x_in.at[b, channels(mp_me)], in_s.at[k - 1, b], in_r.at[mp_me, b], to
        )

    def send_tokens(b, _):
        for k in range(1, n_mp):
            token_copy(k, b).start()
        return 0

    lax.fori_loop(0, images, send_tokens, 0)

    for row, ref in ((0, g1), (1, c1), (2, g2), (3, c2), (4, b2)):
        rows_s[row : row + 1, :] = ref[...].reshape(1, width)
    for j in range(blocks):
        b1_s[j, 0:1, :] = b1[j * BLOCK : (j + 1) * BLOCK].reshape(1, BLOCK)
    rows_s[5:6, 0:hidden] = tb1[...].reshape(1, hidden)
    rows_s[6:7, 0:patches] = tb2[...].reshape(1, patches)
    cols_s[0] = jnp.broadcast_to(rows_s[0:1, :], (128, width)).T
    cols_s[1] = jnp.broadcast_to(rows_s[1:2, :], (128, width)).T
    tw1p[...] = jnp.zeros_like(tw1p)
    tw1p[0:patches, :] = tw1[...]
    tw1t[...] = tw1p[...].T
    tw2t[...] = jnp.zeros_like(tw2t)
    tw2t[0:patches, :] = tw2[...]
    tw2p[...] = tw2t[...].T
    n1_s[...] = jnp.zeros_like(n1_s)
    dm_s[...] = jnp.zeros_like(dm_s)
    va[...] = jnp.zeros_like(va)
    ln1_a[...] = jnp.zeros_like(ln1_a)
    dm_t[...] = jnp.zeros_like(dm_t)
    tg_a[...] = jnp.zeros_like(tg_a)
    cb1_a[...] = jnp.zeros_like(cb1_a)
    v_b[...] = jnp.zeros_like(v_b)

    own_cot.wait()
    for c in range(0, width, 128):
        cols = slice(c, c + 128)
        wide = n2_f[:, cols].astype(F32)
        va[4:5, cols] = jnp.sum(wide, axis=0, keepdims=True)
        lane = c // 128
        dn_a[lane] = wide
        for b in range(images):
            g_f[b * patches : (b + 1) * patches, cols] = dn_a[lane, pl.ds(b, patches, stride=images), :].astype(BF)
    dn_a[...] = jnp.zeros_like(dn_a)

    def transpose_rows(src, dst):
        for lo in range(0, total, 128):
            hi = min(lo + 128, total)
            dst[:, lo:hi] = src[lo:hi, :].T

    transpose_rows(g_f, g_t)

    def token_forward(b, _):
        for k in range(1, n_mp):
            other, to = mp_peer(k)
            remote(
                tokens.at[mp_me * images + b],
                x_in.at[b, channels(other)],
                in_s.at[k - 1, b],
                in_r.at[other, b],
                to,
            ).wait_recv()
        own_tokens(b).wait()
        x = x_in[b].astype(F32)
        xhat, _ = standardize(x, 0)
        n1_s[:, 0:patches] = (xhat * cols_s[0, :, 0:1] + cols_s[1, :, 0:1]).astype(BF)
        act, slope = gelu_both(dot(n1_s[...], tw1p[...]) + rows_s[5:6, 0:hidden])
        act = act.astype(BF)
        act_t[b] = act
        slope_t[b] = slope.astype(BF)
        mixed = dot(act, tw2p[...])[:, 0:patches] + rows_s[6:7, 0:patches]
        dm_t[:, 0:patches] = (x + mixed).astype(BF)
        mid_p[b] = dm_t[...].T[0:patches, :]
        return 0

    lax.fori_loop(0, images, token_forward, 0)

    for b in range(images):
        mid = mid_p[b].astype(F32)
        xhat, _ = standardize(mid, 1)
        rows = slice(b * patches, (b + 1) * patches)
        n2_f[rows, :] = (xhat * rows_s[2:3, :] + rows_s[3:4, :]).astype(BF)
        out_a[rows, :] = mid + rows_s[4:5, :]
    transpose_rows(n2_f, n2_t)

    core = ("mp", 0)
    core_bit = bit_of(core)

    ids = {}
    for s, (_, _, stages) in enumerate(streams):
        for t in range(len(stages)):
            ids[s, t] = 1 + len(ids)
    held = []
    for base, rows, stages in streams:
        line, off = [(base, rows)], base
        for key, have, halved in stages:
            off = off + bit_of(key) * have if halved else off
            line.append((off, have))
        held.append(line)

    def region(s, t, j):
        off, rows = held[s][t]
        if not isinstance(off, int):
            off = pl.multiple_of(off, 16)
        return gw_o.at[core_bit, pl.ds(off, rows), pl.ds(pl.multiple_of(j * BLOCK, BLOCK), BLOCK)]

    def sums(s, t, j):
        ref = rest[ids[s, t] - 1]
        return ref.at[lax.rem(j, ref.shape[0])]

    def source(s, t, j):
        base, _, _ = streams[s]
        return (r0.at[lax.rem(j, SLOTS)], base) if t == 0 else (sums(s, t - 1, j), 0)

    def core_copy(j):
        return remote(part.at[1 - core_bit], r0.at[lax.rem(j, SLOTS)], rs_s.at[0, j], rs_r.at[0, j], partner(core))

    def stage_copy(s, t, j):
        key, rows, halved = streams[s][2][t]
        ref, low = source(s, t, j)
        low = low + (1 - bit_of(key)) * rows if halved else low
        if not isinstance(low, int):
            low = pl.multiple_of(low, 16)
        i = ids[s, t]
        return remote(ref.at[pl.ds(low, rows)], sums(s, t, j), rs_s.at[i, j], rs_r.at[i, j], partner(key))

    def add_rows(dst, src, low, rows):
        chunk = next(c for c in (64, 48, 32, 16) if rows % c == 0)

        def step(i, _):
            here = pl.ds(pl.multiple_of(i * chunk, 16), chunk)
            there = pl.ds(pl.multiple_of(low + i * chunk, 16), chunk)
            dst[here, :] = (dst[here, :].astype(F32) + src[there, :].astype(F32)).astype(BF)
            return 0

        lax.fori_loop(0, rows // chunk, step, 0)

    def finish_core(j):
        core_copy(j).wait()
        add_rows(r0.at[lax.rem(j, SLOTS)], part.at[core_bit], 0, width)

    def finish_stage(s, t, j):
        stage_copy(s, t, j).wait()
        key, rows, halved = streams[s][2][t]
        ref, low = source(s, t, j)
        add_rows(sums(s, t, j), ref, low + bit_of(key) * rows if halved else low, rows)

    gathers = [[t for t in reversed(range(len(stages))) if stages[t][2]] for _, _, stages in streams]

    def own_copy(s, j):
        last = len(streams[s][2])
        return pltpu.make_async_copy(sums(s, last - 1, j), region(s, last, j), own_l.at[s, j])

    def gather_copy(s, a, j):
        t = gathers[s][a]
        key = streams[s][2][t][0]
        here = region(s, t + 1, j)
        src = sums(s, len(streams[s][2]) - 1, j) if a == 0 else here
        i = ids[s, t]
        return remote(src, here, ag_s.at[i, j], ag_r.at[i, j], partner(key))

    def gather_core(j):
        here = gw_o.at[core_bit, :, pl.ds(pl.multiple_of(j * BLOCK, BLOCK), BLOCK)]
        return remote(here, here, ag_s.at[0, j], ag_r.at[0, j], partner(core))

    n_rs = len(streams[0][2])
    n_ag = len(gathers[0])
    every = range(len(streams))

    def advance(step, j):
        if step == 0:
            core_copy(j).start()
        elif step <= n_rs:
            if step == 1:
                finish_core(j)
            else:
                for s in every:
                    finish_stage(s, step - 2, j)
            for s in every:
                stage_copy(s, step - 1, j).start()
        elif step == n_rs + 1:
            for s in every:
                finish_stage(s, n_rs - 1, j)
                own_copy(s, j).start()
                gather_copy(s, 0, j).start()
        elif step <= n_rs + n_ag + 1:
            a = step - n_rs - 1
            for s in every:
                gather_copy(s, a - 1, j).wait()
                if a == 1:
                    own_copy(s, j).wait()
            if a < n_ag:
                for s in every:
                    gather_copy(s, a, j).start()
            else:
                gather_core(j).start()
        else:
            gather_core(j).wait()

    n_steps = n_rs + n_ag + 3
    lags = list(LAGS[:n_steps])
    while len(lags) < n_steps:
        lags.append(lags[-1] + 1)

    def points(i, p):
        for step in reversed(range(n_steps)):
            lag = lags[step] + POINTS - 1
            if lag % POINTS == p:
                j = i - lag // POINTS

                @pl.when((j >= 0) & (j < blocks))
                def _():
                    advance(step, j)

    def unit(h, j):
        slot = lax.rem(j, 2)
        rows = slice(h * half, (h + 1) * half)
        for lo in range(0, BLOCK, 256):
            cols = slice(lo, lo + 256)
            act, slope = gelu_both(dot(n2_f[rows, :], w1_s[slot, :, cols]) + b1_s[j, 0:1, cols])
            act_s[rows, cols] = act.astype(BF)
            dp = dot_nt(g_f[rows, :], w2_s[slot, cols, :]) * slope
            cb1_a[j, 0:1, cols] += jnp.sum(dp, axis=0, keepdims=True)
            dp_s[rows, cols] = dp.astype(BF)
        out_a[rows, :] += dot(act_s[rows, :], w2_s[slot])
        dn = dot_nt(dp_s[rows, :], w1_s[slot])
        for lane in range(width // 128):
            dn_a[lane, rows, :] += dn[:, lane * 128 : (lane + 1) * 128]

    def block_step(j, _):
        for copy in weights(j):
            copy.wait()

        @pl.when(j + 1 < blocks)
        def _():
            for copy in weights(j + 1):
                copy.start()

        unit(0, j)
        points(j, 0)
        unit(1, j)
        points(j, 1)
        part[0] = dot(n2_t[...], dp_s[...]).astype(BF)
        part[1] = dot(g_t[...], act_s[...]).astype(BF)
        points(j, 2)
        return 0

    lax.fori_loop(0, blocks, block_step, 0)

    def grad_copy(k, b):
        other, to = mp_peer(k)
        return remote(
            x_in.at[b, channels(other)], dtok_o.at[mp_me * images + b], out_s.at[k - 1, b], out_r.at[mp_me, b], to
        )

    def own_grad(b):
        return pltpu.make_async_copy(x_in.at[b, channels(mp_me)], dtok_o.at[mp_me * images + b], out_l.at[b])

    def token_backward(t, odd):
        b = 2 * t + odd
        rows = slice(odd * patches, (odd + 1) * patches)
        xhat2, rstd2 = standardize(mid_p[b].astype(F32), 1)
        both = dn_a.at[:, pl.ds(pl.multiple_of(2 * patches * t, 8), 2 * patches)]
        dn2 = jnp.concatenate([both[lane, rows, :] for lane in range(width // 128)], axis=1)
        for q in range(4):

            @pl.when(b % 4 == q)
            def _():
                quad = g_f.at[pl.ds(pl.multiple_of(4 * patches * (b // 4), 16), 4 * patches)]
                g_in[...] = quad[q * patches : (q + 1) * patches, :]

        va[2:3, :] += jnp.sum(dn2 * xhat2, axis=0, keepdims=True)
        va[3:4, :] += jnp.sum(dn2, axis=0, keepdims=True)
        dxh = dn2 * rows_s[2:3, :]
        first = jnp.sum(dxh, axis=-1, keepdims=True) / width
        second = jnp.sum(dxh * xhat2, axis=-1, keepdims=True) / width
        dm_s[0:patches, :] = (g_in[...].astype(F32) + rstd2 * (dxh - first - xhat2 * second)).astype(BF)
        dm_t[...] = dm_s[...].T
        d_mid = dm_t[:, 0:patches].astype(F32)
        va[6:7, 0:patches] += jnp.sum(d_mid, axis=0, keepdims=True)
        d_pre = dot(dm_t[...], tw2t[...]) * slope_t[b].astype(F32)
        va[5:6, 0:hidden] += jnp.sum(d_pre, axis=0, keepdims=True)
        d_pre = d_pre.astype(BF)
        tg_a[SPACE:, :] += dot(dm_s[...], act_t[b])
        xhat1, rstd1 = standardize(x_in[b].astype(F32), 0)
        n1_s[:, 0:patches] = (xhat1 * cols_s[0, :, 0:1] + cols_s[1, :, 0:1]).astype(BF)
        tg_a[0:SPACE, :] += dot(n1_s[...].T, d_pre)
        dn1 = dot(d_pre, tw1t[...])[:, 0:patches]
        ln1_a[:, 0:1] += jnp.sum(dn1 * xhat1, axis=1, keepdims=True)
        ln1_a[:, 1:2] += jnp.sum(dn1, axis=1, keepdims=True)
        dxh = dn1 * cols_s[0, :, 0:1]
        first = jnp.sum(dxh, axis=0, keepdims=True) / width
        second = jnp.sum(dxh * xhat1, axis=0, keepdims=True) / width
        x_in[b] = (d_mid + rstd1 * (dxh - first - xhat1 * second)).astype(BF)
        for k in range(1, n_mp):
            grad_copy(k, b).start()
        own_grad(b).start()

    def wait_tokens(b, _):
        for k in range(1, n_mp):
            token_copy(k, b).wait_send()
        return 0

    lax.fori_loop(0, images, wait_tokens, 0)

    pairs = images // 2
    last_point = POINTS * (blocks - 1) + POINTS - 1 + lags[-1]

    def drain(t, _):
        @pl.when(t < pairs)
        def _():
            token_backward(t, 0)

        points(blocks + t, 0)

        @pl.when(t < pairs)
        def _():
            token_backward(t, 1)

        points(blocks + t, 1)
        points(blocks + t, 2)
        return 0

    lax.fori_loop(0, max(pairs, last_point // POINTS + 1 - blocks), drain, 0)

    for c in range(0, width, 128):
        cols = slice(c, c + 128)
        for b in range(images):
            dn_a[c // 128, pl.ds(b, patches, stride=images), :] = out_a[b * patches : (b + 1) * patches, cols]
        n2_f[:, cols] = dn_a[c // 128].astype(BF)
    own_out = pltpu.make_async_copy(n2_f, out_o, o_l.at[0])
    own_out.start()

    t_rows = t_b.shape[0] // n_mp
    v_rows = v_b.shape[0] // n_mp
    s_rows = t_s2.shape[0]
    t_b[...] = tg_a[...].astype(BF)
    w_v = v_b.shape[1]
    va[0:2, :] = ln1_a[...].T[0:2, :]
    for row in range(7):
        for c in range(width // w_v):
            v_b[row * 2 + c : row * 2 + c + 1, :] = va[row : row + 1, c * w_v : (c + 1) * w_v]
    for c in range(0, blocks * BLOCK, 128):
        row, col = 14 + c // w_v, c % w_v
        v_b[row : row + 1, col : col + 128] = cb1_a[c // BLOCK, 0:1, c % BLOCK : c % BLOCK + 128]

    sem = 0
    copies = []
    for k in range(1, n_mp):
        other, to = mp_peer(k)
        copies.append(
            remote(t_b.at[pl.ds(pl.multiple_of(other * t_rows, 16), t_rows)], t_r1.at[mp_me], sm_s.at[sem], sm_r.at[sem], to)
        )
        copies.append(
            remote(v_b.at[pl.ds(pl.multiple_of(other * v_rows, 8), v_rows)], v_r1.at[mp_me], sm_s.at[sem + 1], sm_r.at[sem + 1], to)
        )
        sem += 2
    for copy in copies:
        copy.start()
    t_r1[mp_me] = t_b[pl.ds(pl.multiple_of(mp_me * t_rows, 16), t_rows), :]
    v_r1[mp_me] = v_b[pl.ds(pl.multiple_of(mp_me * v_rows, 8), v_rows), :]
    for copy in copies:
        copy.wait()
    acc_t, acc_v = t_r1[0].astype(F32), v_r1[0]
    for k in range(1, n_mp):
        acc_t, acc_v = acc_t + t_r1[k].astype(F32), acc_v + v_r1[k]
    t_s1[...] = acc_t.astype(BF)
    v_s1[0] = acc_v

    def spot(i):
        return pl.ds(pl.multiple_of(i * s_rows, 16), s_rows)

    for g, group in enumerate(groups):
        size = group[1]
        mine = member(group)
        copies = []
        for k in range(1, size):
            other, to = peer(group, k)
            src = t_s1.at[spot(other)] if g == 0 else t_s2
            copies.append(remote(src, t_r2.at[g, mine], sm_s.at[sem], sm_r.at[sem], to))
            copies.append(remote(v_s1.at[g], v_r2.at[g, mine], sm_s.at[sem + 1], sm_r.at[sem + 1], to))
            sem += 2
        for copy in copies:
            copy.start()
        t_r2[g, mine] = t_s1[spot(mine)] if g == 0 else t_s2[...]
        v_r2[g, mine] = v_s1[g]
        for copy in copies:
            copy.wait()
        acc_t, acc_v = t_r2[g, 0].astype(F32), v_r2[g, 0]
        for k in range(1, size):
            acc_t, acc_v = acc_t + t_r2[g, k].astype(F32), acc_v + v_r2[g, k]
        t_s2[...] = acc_t.astype(BF)
        v_s1[g + 1] = acc_v

    group = groups[0]
    mine = member(group)
    v_sum = v_s1.at[len(groups)]
    v_here = smv_o.at[pl.ds(pl.multiple_of(mp_me * v_rows, 8), v_rows)]
    t_here = smt_o.at[pl.ds(pl.multiple_of(mp_me * t_rows, 16), t_rows)]
    copies, later = [], []
    for k in range(1, group[1]):
        _, to = peer(group, k)
        copies.append(remote(t_s2, t_g.at[spot(mine)], sm_s.at[sem], sm_r.at[sem], to))
        sem += 1
    for k in range(1, n_mp):
        _, to = mp_peer(k)
        later.append(remote(v_sum, v_here, sm_s.at[sem], sm_r.at[sem], to))
        sem += 1
    for copy in copies + later:
        copy.start()
    v_own = pltpu.make_async_copy(v_sum, v_here, sm_l.at[0])
    v_own.start()
    t_g[spot(mine)] = t_s2[...]
    for copy in copies:
        copy.wait()
    for k in range(1, n_mp):
        _, to = mp_peer(k)
        copy = remote(t_g, t_here, sm_s.at[sem], sm_r.at[sem], to)
        copy.start()
        later.append(copy)
        sem += 1
    t_own = pltpu.make_async_copy(t_g, t_here, sm_l.at[1])
    t_own.start()
    v_own.wait()
    t_own.wait()
    for copy in later:
        copy.wait()

    def wait_grads(b, _):
        for k in range(1, n_mp):
            other, to = mp_peer(k)
            grad_copy(k, b).wait_send()
            remote(
                x_in.at[b, channels(other)],
                dtok_o.at[other * images + b],
                out_s.at[k - 1, b],
                out_r.at[other, b],
                to,
            ).wait_recv()
        own_grad(b).wait()
        return 0

    lax.fori_loop(0, images, wait_grads, 0)
    own_out.wait()


def body(tokens, cot, g1, c1, tw1, tb1, tw2, tb2, g2, c2, w1, b1, w2, b2):
    n_mp, n_dp = lax.axis_size("mp"), lax.axis_size("dp")
    images, patches, width = cot.shape
    hidden = tw1.shape[1]
    local = tokens.shape[2]
    deep = w1.shape[1]
    tokens = tokens.transpose(0, 2, 1)
    cot = cot.transpose(1, 0, 2).reshape(patches * images, width)
    tw2 = tw2.T
    blocks = deep // BLOCK
    streams = reduce_plan(n_mp, n_dp, width)
    groups = dp_groups(n_dp)
    total = images * patches
    half_w = width // 2
    stage_rows = [(4 if t == 0 else blocks, have) for _, _, stages in streams for t, (_, have, _) in enumerate(stages)]
    n_ids = 1 + len(stage_rows)
    n_small = 2 * (n_mp - 1) + sum(2 * (size - 1) for _, size in groups) + groups[0][1] - 1 + 2 * (n_mp - 1)
    t_rows = 2 * SPACE // n_mp
    s_rows = t_rows // groups[0][1]
    hbm, vmem = pl.BlockSpec(memory_space=pl.ANY), pl.BlockSpec(memory_space=pltpu.VMEM)
    dma = pltpu.SemaphoreType.DMA
    scratch = [
        pltpu.VMEM((images, width, patches), BF),
        pltpu.VMEM((patches, width), BF),
        pltpu.VMEM((images, patches, width), BF),
        pltpu.VMEM((total, width), BF),
        pltpu.VMEM((width, total), BF),
        pltpu.VMEM((total, width), BF),
        pltpu.VMEM((width, total), BF),
        pltpu.VMEM((images, width, hidden), BF),
        pltpu.VMEM((images, width, hidden), BF),
        pltpu.VMEM((total, width), F32),
        pltpu.VMEM((width // 128, total, 128), F32),
        pltpu.VMEM((total, BLOCK), BF),
        pltpu.VMEM((total, BLOCK), BF),
        pltpu.VMEM((2, width, BLOCK), BF),
        pltpu.VMEM((2, BLOCK, width), BF),
        pltpu.VMEM((2, width, BLOCK), BF),
        pltpu.VMEM((SLOTS, width, BLOCK), BF),
        [pltpu.VMEM((min(keep, blocks), rows, BLOCK), BF) for keep, rows in stage_rows],
        pltpu.VMEM((width, SPACE), BF),
        pltpu.VMEM((SPACE, width), BF),
        pltpu.VMEM((width, SPACE), BF),
        pltpu.VMEM((SPACE, hidden), BF),
        pltpu.VMEM((hidden, SPACE), BF),
        pltpu.VMEM((hidden, SPACE), BF),
        pltpu.VMEM((SPACE, hidden), BF),
        pltpu.VMEM((8, width), F32),
        pltpu.VMEM((blocks, 8, BLOCK), F32),
        pltpu.VMEM((2, width, 128), F32),
        pltpu.VMEM((blocks, 8, BLOCK), F32),
        pltpu.VMEM((8, width), F32),
        pltpu.VMEM((width, 128), F32),
        pltpu.VMEM((2 * SPACE, hidden), F32),
        pltpu.VMEM((2 * SPACE, hidden), BF),
        pltpu.VMEM((n_mp, t_rows, hidden), BF),
        pltpu.VMEM((t_rows, hidden), BF),
        pltpu.VMEM((len(groups), groups[0][1], s_rows, hidden), BF),
        pltpu.VMEM((s_rows, hidden), BF),
        pltpu.VMEM((t_rows, hidden), BF),
        pltpu.VMEM((8 * n_mp, half_w), F32),
        pltpu.VMEM((n_mp, 8, half_w), F32),
        pltpu.VMEM((len(groups) + 1, 8, half_w), F32),
        pltpu.VMEM((len(groups), groups[0][1], 8, half_w), F32),
        dma((n_mp - 1, images)),
        dma((n_mp, images)),
        dma((images,)),
        dma((1,)),
        dma((2, 2)),
        dma((1,)),
        dma((n_mp - 1, images)),
        dma((n_mp, images)),
        dma((images,)),
        dma((n_ids, blocks)),
        dma((n_ids, blocks)),
        dma((n_ids, blocks)),
        dma((n_ids, blocks)),
        dma((len(streams), blocks)),
        dma((n_small,)),
        dma((n_small,)),
        dma((2,)),
    ]
    out, dtok, gw, smt, smv = pl.pallas_call(
        functools.partial(layer_kernel, n_mp, n_dp, streams, groups),
        out_shape=(
            jax.ShapeDtypeStruct(cot.shape, BF),
            jax.ShapeDtypeStruct(tokens.shape, BF),
            jax.ShapeDtypeStruct((2, width, deep), BF),
            jax.ShapeDtypeStruct((2 * SPACE, hidden), BF),
            jax.ShapeDtypeStruct((8 * n_mp, half_w), F32),
        ),
        in_specs=[hbm] * 4 + [vmem] * 10,
        out_specs=(hbm,) * 5,
        scratch_shapes=scratch,
        compiler_params=pltpu.CompilerParams(
            collective_id=0, has_side_effects=True, vmem_limit_bytes=64 * 2**20 - 2**16
        ),
    )(tokens, cot, w1, w2, g1, c1, tw1, tb1, tw2, tb2, g2, c2, b1, b2)
    vec = smv.reshape(-1)
    last = 7 * width
    return (
        out.reshape(patches, images, width).transpose(1, 0, 2),
        dtok.transpose(0, 2, 1),
        vec[0:width],
        vec[width : 2 * width],
        smt[0:patches].astype(F32),
        vec[5 * width : 5 * width + hidden],
        smt[SPACE : SPACE + patches].astype(F32).T,
        vec[6 * width : 6 * width + patches],
        vec[2 * width : 3 * width],
        vec[3 * width : 4 * width],
        gw[0].astype(F32),
        vec[last : last + deep],
        gw[1].T.astype(F32),
        vec[4 * width : 5 * width],
    )


def solution(mesh):
    placed = (P("dp", None, "mp"), P(("dp", "mp"), None, None)) + (P(),) * 12
    return jax.shard_map(body, mesh=mesh, in_specs=placed, out_specs=(placed[1], placed[0]) + (P(),) * 12, check_vma=False)
```

time: 670 us -> 245 us (0.37); the launches traced: 660 us -> 244 us
  waiting for transfers between devices: 211 us -> 0 us
  Pallas kernels: 0 us -> 209 us
  matrix products: 203 us -> 0 us
  blocking collectives: 67.8 us -> 0 us
  local copies, waits for them, and re-layouts: 87.8 us -> 21.2 us
  starting transfers between devices: 33 us -> 0 us
  other arithmetic: 41.8 us -> 13.7 us
  between operations: 16.1 us -> 0.67 us
    pallas_call x0 -> x1, Pallas kernels: none -> 209 us  [body(): pl.pallas_call(functools.partial(layer_kernel, n_mp, n_dp, streams, group...]
    dot_general x48 -> x0, matrix products: 203 us -> none  [the longest x4 35.6 us: channel_pass(): jnp.einsum('rc,rh->ch', upstream_rows, act_chan, preferred_element_type=j...]
    psum x1 -> x0, waiting for transfers between devices: 196 us -> none  [body(): lax.psum((acc_ln1[0], acc_ln1[1], acc_tok[0], acc_tok[1], acc_tok[2], acc...]
    psum x3 -> x0, blocking collectives: 67.8 us -> none  [the longest x1 42.3 us: body(): lax.psum((acc_ln1[0], acc_ln1[1], acc_tok[0], acc_tok[1], acc_tok[2], acc...]
    all_to_all x8 -> x0, starting transfers between devices: 32.9 us -> none  [the longest x4 17 us: body(): lax.all_to_all(middle_gradient, 'mp', split_axis=2, concat_axis=0, tiled=...]
    reshape x16 -> x1, local copies, waits for them, and re-layouts: 24.7 us -> 0.8 us  [body(): vec = smv.reshape(-1)]
    reduce_sum x13 -> x0, other arithmetic: 22.8 us -> none  [the longest x4 7.47 us: channel_pass(): mean_value = jnp.sum(value_entries, axis=-1, keepdims=True) / feature_width]
    all_to_all x8 -> x0, waiting for transfers between devices: 14.7 us -> none  [the longest x4 8.89 us: body(): rows = lax.all_to_all(mid, 'mp', split_axis=0, concat_axis=2, tiled=True)]
  transfers between devices with their start and end apart: 9 -> 0, of which waited for: 5 -> 0; matrix products, arithmetic and copies ran while one was open for 36% -> 0% of each run, Pallas kernels for 0% -> 0%
where the time goes in v1:
time: 245 us; the launch traced here: 244 us
  Pallas kernels  209 us (85%)
  local copies, waits for them, and re-layouts  21.2 us (9%)
  other arithmetic  13.7 us (6%)
    pallas_call x1, Pallas kernels, body(): pl.pallas_call(functools.partial(layer_kernel, n_mp, n_dp, streams, group...  209 us
    unnamed x9, local copies, waits for them, and re-layouts  13.4 us
    convert_element_type x1, other arithmetic, body(): gw[1].T.astype(F32)  12.8 us

profile of v1, /device:TPU:0, one launch (start us, length us, event | category | flops | bytes accessed | tf_op | source)
XLA Modules:
  0.0 244.4 jit_solution(10522114611800690372)
XLA Ops:
  0.7 208.8 %shard_map.245 = (bf16[1568,768]{1,0:T(8,128)(2,1)}, bf16[32,192,196]{2,1,0:T(8,128)(2,1)}, bf16[2,768,3072]{2,1,0:T(8,128)(2,1)}, bf16[512,384]{1,0:T(8,128)(2,1)}, f32[32,384]{1,0:T(8,128)}) custom-call(bf16[32,192,196]{2,1,0:T(8,128)(2,1)} %bitcast.19, bf16[1568,768]{1,0:T(8,128)(2,1)} %bitcast.21, bf16[768,3072]{1,0:T(8,128)(2,1)} %w1.1, ...), custom_call_target="tpu_custom_call" | custom-call | tf_op jit(solution)/shard_map/pallas_call | solution.py:765
  209.5 0.9 fusion
  210.3 0.6 slice.58
  210.9 0.6 slice.60
  211.5 0.6 slice.67
  212.1 0.6 slice.69
  212.7 0.6 slice.75
  213.3 0.8 reshape.50
  214.1 0.6 slice.76
  214.7 0.7 slice.71
  215.4 0.6 slice.72
  216.0 1.3 slice_reduce_fusion
  217.3 12.8 %convert_bitcast_fusion = (f32[3072,768]{0,1:T(8,128)}, f32[768,3072]{1,0:T(8,128)}) fusion(bf16[2,768,3072]{2,1,0:T(8,128)(2,1)} %get-tuple-element.23), kind=kLoop, calls=%fused_computation | loop fusion | flops 4718592 | bytes 28311552 | tf_op jit(solution)/shard_map/convert_element_type | solution.py:796
  230.1 0.0 copy-start.2
  230.1 0.0 copy-start.1
  230.1 9.7 %copy.28 = f32[3072,768]{1,0:T(8,128)} copy(f32[3072,768]{0,1:T(8,128)} %get-tuple-element.38) | data formatting | bytes 18874368
  239.9 0.0 copy-start
  239.9 0.0 copy-done.2
  239.9 0.9 convert_bitcast_fusion.1
  240.7 0.0 copy-done.1
  240.7 1.4 copy.31
  242.2 0.5 copy-done
  242.7 1.7 copy.32
Async XLA Ops:
  230.1 9.7 %copy-start.2 = (bf16[512,384]{1,0:T(8,128)(2,1)S(1)}, bf16[512,384]{1,0:T(8,128)(2,1)}, u32[]{:S(2)}) copy-start(bf16[512,384]{1,0:T(8,128)(2,1)} %get-tuple-element.22) | copy-start | bytes 1179652
  230.1 10.6 %copy-start.1 = (bf16[1568,768]{1,0:T(8,128)(2,1)S(1)}, bf16[1568,768]{1,0:T(8,128)(2,1)}, u32[]{:S(2)}) copy-start(bf16[1568,768]{1,0:T(8,128)(2,1)} %get-tuple-element.19) | copy-start | bytes 7225348
  239.9 2.8 %copy-start = (bf16[32,192,196]{2,1,0:T(8,128)(2,1)S(1)}, bf16[32,192,196]{2,1,0:T(8,128)(2,1)}, u32[]{:S(2)}) copy-start(bf16[32,192,196]{2,1,0:T(8,128)(2,1)} %get-tuple-element.20) | copy-start | bytes 7225348

commit v2 on v1

v2 whole, which is shorter than its diff:
```python
import functools

import jax
import jax.numpy as jnp
from jax import lax
from jax.experimental import pallas as pl
from jax.experimental.pallas import tpu as pltpu
from jax.sharding import PartitionSpec as P

BF = jnp.bfloat16
F32 = jnp.float32
EPS = 1e-06
MESH = pl.DeviceIdType.MESH
NT = (((1,), (1,)), ((), ()))

BLOCK = 512
ROW = 200
VMEM_LIMIT = 64 * 2**20 - 2**16
SPACE = 256
PLAN = (
    (),
    (),
    (10000,),
    (),
    (10100, 20000, 30000, 40000),
    (),
    (10200, 20001, 30001, 40001, 20100, 40100),
    (30002, 30100, 20002),
    (10300, 40002, 20101, 40101, 20200, 30003, 40200, 20003, 30200),
    (40003, 30101),
    (10400, 20102, 30102, 40102, 20201, 30201, 40201, 20300, 30300, 20004, 30004, 40004),
    (20103, 40103, 40300, 30103, 30202),
    (10500, 20202, 20301, 20400, 30400, 30005, 40104, 40202, 40301, 20005),
    (20203, 30203, 40203, 20500, 40005, 20104, 30301, 20401, 30104),
    (40401, 30402, 20403, 20502, 20007, 20106, 20205, 30501, 30106, 40206, 20304, 30304),
    (20302, 40302, 30302, 30500, 20006, 30105, 40105, 40204),
    (40303, 20501, 40006, 20204, 30204),
    (20303, 30303, 40400, 30401, 20402, 30006, 20105, 40106, 40304),
    (30205, 40205),
    (40500, 30007, 20008, 40305),
    (30403, 20503, 30008, 20206, 30206, 30502, 20404),
    (40402, 40501, 40007, 30107, 20305, 30305, 40306),
    (30503, 40008, 40107, 30108, 30207, 30404, 20405, 20504),
    (40403, 40502, 40108, 40207, 30208, 20306, 30306, 20406, 30504, 20505),
    (40208, 40307, 30405, 20506),
    (40503, 20107, 30307, 40308, 40404),
    (30406, 20108, 30308, 30505, 40405, 40504, 30407, 30506, 40406, 30408, 40505, 20207, 30507, 20208, 40407, 40506, 30508, 40408, 40507, 20307, 20407, 20507, 40508, 20308, 20408, 20508),
)


def dot(a, b):
    return jnp.dot(a, b, preferred_element_type=F32)


def dot_nt(a, b):
    return lax.dot_general(a, b, NT, preferred_element_type=F32)


def gelu_both(v):
    cdf = 0.5 + 0.5 * lax.erf(v * 0.7071067811865476)
    return v * cdf, cdf + v * (jnp.exp(-0.5 * v * v) * 0.3989422804014327)


def standardize(v, axis):
    width = v.shape[axis]
    mean = jnp.sum(v, axis=axis, keepdims=True) / width
    square = jnp.sum(v * v, axis=axis, keepdims=True) / width
    rstd = lax.rsqrt(square - mean * mean + EPS)
    return (v - mean) * rstd, rstd


def bits_of(n):
    return n.bit_length() - 1


def reduce_plan(n_mp, n_dp, width):
    dp = [("dp", b) for b in range(bits_of(n_dp))]
    mp = [("mp", b) for b in range(1, bits_of(n_mp))]
    if len(dp) == 3 and len(mp) == 1:
        third = width // 3
        orders = ([mp[0], dp[0], dp[1], dp[2]], [dp[0], dp[1], mp[0], dp[2]], [dp[1], dp[0], dp[2], mp[0]])
        raw = [(s * third, third, order) for s, order in enumerate(orders)]
    else:
        raw = [(0, width, dp + mp)]
    streams = []
    for base, rows, keys in raw:
        stages, have = [], rows
        for key in keys:
            halved = have % 32 == 0
            have = have // 2 if halved else have
            stages.append((key, have, halved))
        streams.append((base, rows, stages))
    return streams


def small_groups(n_mp, n_dp):
    size = min(8, n_dp)
    groups, stride = [(1, size, n_mp // 2)], size
    while stride < n_dp:
        size = min(8, n_dp // stride)
        groups.append((stride, size, 1))
        stride *= size
    return groups


def plan_steps(blocks, images, streams):
    pieces = [("block", j, p) for j in range(blocks) for p in range(2)] + [("loop",)] + [("dense", h) for h in range(2)]
    pieces += [("image", b) for b in range(images)] + [("out", h) for h in range(2)] + [("end",)]
    if len(streams) == 3 and len(PLAN) == len(pieces) + 1:
        return dict(zip(pieces, PLAN)), PLAN[-1]
    table = {piece: [] for piece in pieces}
    for j in range(blocks):
        table[("block", j + 1, 0) if j + 1 < blocks else ("loop",)].append(10000 + 100 * j)
    last = max(len(stages) + sum(halved for _, _, halved in stages) for _, _, stages in streams)
    return table, [20000 + 10000 * s + 100 * j + k for k in range(last + 1) for j in range(blocks) for s in range(len(streams))]


def layer_kernel(
    n_mp,
    n_dp,
    streams,
    groups,
    tokens,
    cot,
    w1,
    w2,
    g1,
    c1,
    tw1,
    tb1,
    tw2,
    tb2,
    g2,
    c2,
    b1,
    b2,
    out_o,
    dtok_o,
    gw_o,
    smt_o,
    tok_h,
    hid_h,
    x_in,
    g_in,
    mid_p,
    g_f,
    n2_f,
    wide_s,
    tok_s,
    dn_a,
    dm_a,
    mix_s,
    hid_s,
    w1_s,
    w2_s,
    part,
    r0,
    rest,
    n1_s,
    dm_s,
    dm_t,
    tw1p,
    tw1t,
    tw2p,
    tw2t,
    rows_s,
    b1_s,
    cols_s,
    cb1_a,
    va,
    ln1_a,
    tg_a,
    t_b,
    t_r1,
    t_r2,
    t_s2,
    t_g,
    in_s,
    in_r,
    in_l,
    g_l,
    w_l,
    o_l,
    tok_l,
    hid_l,
    wide_l,
    out_s,
    out_r,
    out_l,
    rs_s,
    rs_r,
    ag_s,
    ag_r,
    own_l,
    sm_s,
    sm_r,
    sm_l,
):
    images, width, patches = x_in.shape
    local = tokens.shape[1]
    hidden = tw1.shape[1]
    blocks = w1.shape[1] // BLOCK
    total = images * patches
    half = total // 2
    mp_me = lax.axis_index("mp")
    dp_me = lax.axis_index("dp")

    def bit_of(key):
        axis, b = key
        me = mp_me if axis == "mp" else dp_me
        return (me // (1 << b)) % 2

    def partner(key):
        axis, b = key
        me = mp_me if axis == "mp" else dp_me
        return {axis: me + (1 << b) * (1 - 2 * bit_of(key))}

    def member(group):
        stride, size, across = group
        index = (dp_me // stride) % size
        return index * across + mp_me // 2 if across > 1 else index

    def peer(group, k):
        stride, size, across = group
        mine = member(group)
        other = lax.rem(mine + k, size * across)
        to = {"dp": dp_me + (other // across - (dp_me // stride) % size) * stride}
        if across > 1:
            to["mp"] = (other % across) * 2 + mp_me % 2
        return other, to

    def mp_peer(k):
        other = lax.rem(mp_me + k, n_mp)
        return other, {"mp": other}

    def remote(src, dst, send, recv, to):
        return pltpu.make_async_remote_copy(
            src_ref=src, dst_ref=dst, send_sem=send, recv_sem=recv, device_id=to, device_id_type=MESH
        )

    barrier = pltpu.get_barrier_semaphore()
    greet = [peer(group, k)[1] for group in groups for k in range(1, group[1] * group[2])]
    greet += [{"mp": (mp_me // 2 + k) % (n_mp // 2) * 2 + 1 - mp_me % 2} for k in range(n_mp // 2)]
    for to in greet:
        pl.semaphore_signal(barrier, inc=1, device_id=to, device_id_type=MESH)

    def channels(member):
        return pl.ds(pl.multiple_of(member * local, 16), local)

    def own_tokens(b):
        return pltpu.make_async_copy(tokens.at[mp_me * images + b], x_in.at[b, channels(mp_me)], in_l.at[b])

    own_cot = pltpu.make_async_copy(cot, n2_f, g_l.at[0])

    weights = (
        pltpu.make_async_copy(w1, w1_s, w_l.at[0]),
        pltpu.make_async_copy(w2, w2_s, w_l.at[1]),
    )

    def load_own(b, _):
        own_tokens(b).start()
        return 0

    own_cot.start()
    lax.fori_loop(0, images, load_own, 0)
    pl.semaphore_wait(barrier, len(greet))

    def token_copy(k, b):
        other, to = mp_peer(k)
        return remote(
            tokens.at[other * images + b], x_in.at[b, channels(mp_me)], in_s.at[k - 1, b], in_r.at[mp_me, b], to
        )

    def send_tokens(b, _):
        for k in range(1, n_mp):
            token_copy(k, b).start()
        return 0

    lax.fori_loop(0, images, send_tokens, 0)
    for copy in weights:
        copy.start()

    for row, ref in ((0, g1), (1, c1), (2, g2), (3, c2), (4, b2)):
        rows_s[row : row + 1, :] = ref[...].reshape(1, width)
    for j in range(blocks):
        b1_s[j, 0:1, :] = b1[j * BLOCK : (j + 1) * BLOCK].reshape(1, BLOCK)
    rows_s[5:6, 0:hidden] = tb1[...].reshape(1, hidden)
    rows_s[6:7, 0:patches] = tb2[...].reshape(1, patches)
    cols_s[0] = jnp.broadcast_to(rows_s[0:1, :], (128, width)).T
    cols_s[1] = jnp.broadcast_to(rows_s[1:2, :], (128, width)).T
    tw1p[...] = jnp.zeros_like(tw1p)
    tw1p[0:patches, :] = tw1[...]
    tw1t[...] = tw1p[...].T
    tw2t[...] = jnp.zeros_like(tw2t)
    tw2t[0:patches, :] = tw2[...]
    tw2p[...] = tw2t[...].T
    n1_s[...] = jnp.zeros_like(n1_s)
    dm_s[...] = jnp.zeros_like(dm_s)
    va[...] = jnp.zeros_like(va)
    ln1_a[...] = jnp.zeros_like(ln1_a)
    dm_t[...] = jnp.zeros_like(dm_t)
    tg_a[...] = jnp.zeros_like(tg_a)
    cb1_a[...] = jnp.zeros_like(cb1_a)

    own_cot.wait()
    for c in range(0, width, 128):
        cols = slice(c, c + 128)
        wide = n2_f[:, cols].astype(F32)
        va[4:5, cols] = jnp.sum(wide, axis=0, keepdims=True)
        mix_s[...] = wide
        for b in range(images):
            g_f[b * patches : (b + 1) * patches, cols] = mix_s[pl.ds(b, patches, stride=images), :].astype(BF)

    aside = -(-total // 128) * 128

    def transpose_rows(src, at):
        for lo in range(0, total, 128):
            hi = min(lo + 128, total)
            wide_s[0:width, at + lo : at + hi] = src[lo:hi, :].T

    transpose_rows(g_f, aside)

    def token_save(b):
        return pltpu.make_async_copy(tok_s.at[lax.rem(b, 2)], tok_h.at[b], tok_l.at[0, lax.rem(b, 2)])

    def token_load(b):
        return pltpu.make_async_copy(tok_h.at[b], tok_s.at[lax.rem(b, 2)], tok_l.at[1, lax.rem(b, 2)])

    def token_forward(b, _):
        for k in range(1, n_mp):
            other, to = mp_peer(k)
            remote(
                tokens.at[mp_me * images + b],
                x_in.at[b, channels(other)],
                in_s.at[k - 1, b],
                in_r.at[other, b],
                to,
            ).wait_recv()
        own_tokens(b).wait()
        x = x_in[b].astype(F32)
        xhat, _ = standardize(x, 0)
        n1_s[:, 0:patches] = (xhat * cols_s[0, :, 0:1] + cols_s[1, :, 0:1]).astype(BF)
        act, slope = gelu_both(dot(n1_s[...], tw1p[...]) + rows_s[5:6, 0:hidden])
        act = act.astype(BF)

        @pl.when(b >= 2)
        def _():
            token_save(b - 2).wait()

        slot = lax.rem(b, 2)
        tok_s[slot, 0] = act
        tok_s[slot, 1] = slope.astype(BF)
        token_save(b).start()
        mixed = dot(act, tw2p[...])[:, 0:patches] + rows_s[6:7, 0:patches]
        dm_t[:, 0:patches] = (x + mixed).astype(BF)
        mid_p[b] = dm_t[...].T[0:patches, :]
        return 0

    def second_norm(h):
        for b in range(h * images // 2, (h + 1) * images // 2):
            xhat, _ = standardize(mid_p[b].astype(F32), 1)
            n2_f[b * patches : (b + 1) * patches, :] = (xhat * rows_s[2:3, :] + rows_s[3:4, :]).astype(BF)

    def unit(h, j):
        slot = lax.rem(j, 2)
        rows = slice(h * half, (h + 1) * half)
        for lo in range(0, BLOCK, 256):
            here = pl.ds(pl.multiple_of(j * BLOCK + lo, 256), 256)
            cols = slice(lo, lo + 256)
            act, slope = gelu_both(dot(n2_f[rows, :], w1_s[:, here]) + b1_s[j, 0:1, cols])
            hid_s[slot, 0, rows, cols] = act.astype(BF)
            dp = dot_nt(g_f[rows, :], w2_s[here, :]) * slope
            cb1_a[j, 0:1, cols] += jnp.sum(dp, axis=0, keepdims=True)
            hid_s[slot, 1, rows, cols] = dp.astype(BF)

    def hidden_copies(kind, h, j):
        slot = lax.rem(j, 2)
        rows = pl.ds(h * half, half)
        cols = pl.ds(pl.multiple_of(j * BLOCK, BLOCK), BLOCK)
        pairs = [(hid_s.at[slot, i, rows, :], hid_h.at[i, rows, cols]) for i in range(2)]
        return [
            pltpu.make_async_copy(here if kind == 0 else there, there if kind == 0 else here, hid_l.at[kind, h, i, slot])
            for i, (here, there) in enumerate(pairs)
        ]

    def start(copies):
        for copy in copies:
            copy.start()

    def wait(copies):
        for copy in copies:
            copy.wait()

    lax.fori_loop(0, images // 2, token_forward, 0)
    second_norm(0)
    wait(weights)

    def early(j, _):
        @pl.when(j >= 2)
        def _():
            wait(hidden_copies(0, 0, j - 2))

        unit(0, j)
        start(hidden_copies(0, 0, j))

        @pl.when(j < images // 2)
        def _():
            token_forward(images // 2 + j, 0)

        return 0

    lax.fori_loop(0, blocks, early, 0)
    for j in range(blocks - 2, blocks):
        wait(hidden_copies(0, 0, j))
    start(hidden_copies(1, 0, 0))
    for b in range(images - 2, images):
        token_save(b).wait()
    second_norm(1)
    transpose_rows(n2_f, 0)

    core = ("mp", 0)
    core_bit = bit_of(core)

    ids = {}
    for s, (_, _, stages) in enumerate(streams):
        for t in range(len(stages)):
            ids[s, t] = 1 + len(ids)
    held = []
    for base, rows, stages in streams:
        line, off = [(base, rows)], base
        for key, have, halved in stages:
            off = off + bit_of(key) * have if halved else off
            line.append((off, have))
        held.append(line)

    def region(s, t):
        off, rows = held[s][t]
        return pl.ds(off if isinstance(off, int) else pl.multiple_of(off, 16), rows)

    def sums(s, t, j):
        return rest[ids[s, t] - 1].at[j]

    def source(s, t, j):
        base, _, _ = streams[s]
        return (r0.at[j], base) if t == 0 else (sums(s, t - 1, j), 0)

    def core_copy(j):
        return remote(part.at[1 - core_bit], r0.at[j], rs_s.at[0, j], rs_r.at[0, j], partner(core))

    def stage_copy(s, t, j):
        key, rows, halved = streams[s][2][t]
        ref, low = source(s, t, j)
        low = low + (1 - bit_of(key)) * rows if halved else low
        if not isinstance(low, int):
            low = pl.multiple_of(low, 16)
        i = ids[s, t]
        return remote(ref.at[pl.ds(low, rows)], sums(s, t, j), rs_s.at[i, j], rs_r.at[i, j], partner(key))

    def add_rows(dst, src, low, rows, into=None, at=0):
        chunk = next(c for c in (64, 48, 32, 16) if rows % c == 0)

        def step(i, _):
            here = pl.ds(pl.multiple_of(i * chunk, 16), chunk)
            there = pl.ds(pl.multiple_of(low + i * chunk, 16), chunk)
            result = (dst[here, :].astype(F32) + src[there, :].astype(F32)).astype(BF)
            if into is None:
                dst[here, :] = result
            else:
                into[pl.ds(pl.multiple_of(at + i * chunk, 16), chunk), :] = result
            return 0

        lax.fori_loop(0, rows // chunk, step, 0)

    def finish_core(j):
        core_copy(j).wait()
        add_rows(r0.at[j], part.at[core_bit], 0, width)

    def finish_stage(s, t, j):
        stage_copy(s, t, j).wait()
        key, rows, halved = streams[s][2][t]
        ref, low = source(s, t, j)
        low = low + bit_of(key) * rows if halved else low
        if t == n_rs - 1:
            add_rows(sums(s, t, j), ref, low, rows, r0.at[j], held[s][n_rs][0])
        else:
            add_rows(sums(s, t, j), ref, low, rows)

    gathers = [[t for t in reversed(range(len(stages))) if stages[t][2]] for _, _, stages in streams]

    def own_copy(s, j):
        base, rows, _ = streams[s]
        there = gw_o.at[core_bit, pl.ds(base, rows), pl.ds(j * BLOCK, BLOCK)]
        return pltpu.make_async_copy(r0.at[j, pl.ds(base, rows), :], there, own_l.at[s, j])

    def gather_copy(s, a, j):
        t = gathers[s][a]
        key = streams[s][2][t][0]
        here = r0.at[j, region(s, t + 1), :]
        i = ids[s, t]
        return remote(here, here, ag_s.at[i, j], ag_r.at[i, j], partner(key))

    def gather_core(s, j):
        base, rows, _ = streams[s]
        there = gw_o.at[core_bit, pl.ds(base, rows), pl.ds(j * BLOCK, BLOCK)]
        i = 1 + len(ids) + s
        return remote(r0.at[j, pl.ds(base, rows), :], there, ag_s.at[i, j], ag_r.at[i, j], partner(core))

    n_rs = len(streams[0][2])
    every = range(len(streams))

    def advance(item):
        s, j, k = item // 10000 - 2, item // 100 % 100, item % 100
        if s < 0:
            finish_core(j)
            for s in every:
                stage_copy(s, 0, j).start()
            return
        n_ag = len(gathers[s])
        if k < n_rs:
            finish_stage(s, k, j)
        elif k < n_rs + n_ag:
            gather_copy(s, k - n_rs, j).wait()
        else:
            gather_core(s, j).wait()
            own_copy(s, j).wait()
        k += 1
        if k < n_rs:
            stage_copy(s, k, j).start()
        elif k < n_rs + n_ag:
            gather_copy(s, k - n_rs, j).start()
        elif k == n_rs + n_ag:
            gather_core(s, j).start()
            own_copy(s, j).start()

    table, rest_steps = plan_steps(blocks, images, streams)

    def slot_steps(items):
        for item in items:
            advance(item)

    def block_step(j, _):
        wait(hidden_copies(1, 0, j))

        @pl.when(j >= 2)
        def _():
            wait(hidden_copies(0, 1, j - 2))

        unit(1, j)
        start(hidden_copies(0, 1, j))

        @pl.when(j + 1 < blocks)
        def _():
            start(hidden_copies(1, 0, j + 1))

        for k in range(blocks):
            if table["block", k, 0]:
                pl.when(j == k)(functools.partial(slot_steps, table["block", k, 0]))
        slot = lax.rem(j, 2)
        part[0] = dot(wide_s[0:width, 0:total], hid_s[slot, 1]).astype(BF)
        part[1] = dot(wide_s[0:width, aside : aside + total], hid_s[slot, 0]).astype(BF)
        core_copy(j).start()
        for k in range(blocks):
            if table["block", k, 1]:
                pl.when(j == k)(functools.partial(slot_steps, table["block", k, 1]))
        return 0

    lax.fori_loop(0, blocks, block_step, 0)
    slot_steps(table["loop",])
    for j in range(blocks - 2, blocks):
        wait(hidden_copies(0, 1, j))

    deep = blocks * BLOCK

    def wide_load(i, h):
        return pltpu.make_async_copy(hid_h.at[i, pl.ds(h * half, half)], wide_s.at[:, pl.ds(0, deep)], wide_l.at[i, h])

    wide_load(1, 0).start()
    token_load(0).start()

    def grad_copy(k, b):
        other, to = mp_peer(k)
        return remote(
            x_in.at[b, channels(other)], dtok_o.at[mp_me * images + b], out_s.at[k - 1, b], out_r.at[mp_me, b], to
        )

    def own_grad(b):
        return pltpu.make_async_copy(x_in.at[b, channels(mp_me)], dtok_o.at[mp_me * images + b], out_l.at[b])

    def token_backward(b, _):
        q = lax.rem(b, images // 2)

        @pl.when(b + 1 < images)
        def _():
            token_load(b + 1).start()

        xhat2, rstd2 = standardize(mid_p[b].astype(F32), 1)
        for i in range(images // 2):

            @pl.when(q == i)
            def _():
                quad = g_f.at[pl.ds(pl.multiple_of(half * (b // (images // 2)), 16), half)]
                g_in[...] = quad[i * patches : (i + 1) * patches, :]
                dm_a[...] = dn_a[i * patches : (i + 1) * patches, :]

        dn2 = dm_a[...]
        va[2:3, :] += jnp.sum(dn2 * xhat2, axis=0, keepdims=True)
        va[3:4, :] += jnp.sum(dn2, axis=0, keepdims=True)
        dxh = dn2 * rows_s[2:3, :]
        first = jnp.sum(dxh, axis=-1, keepdims=True) / width
        second = jnp.sum(dxh * xhat2, axis=-1, keepdims=True) / width
        dm_s[0:patches, :] = (g_in[...].astype(F32) + rstd2 * (dxh - first - xhat2 * second)).astype(BF)
        dm_t[...] = dm_s[...].T
        d_mid = dm_t[:, 0:patches].astype(F32)
        va[6:7, 0:patches] += jnp.sum(d_mid, axis=0, keepdims=True)
        token_load(b).wait()
        slot = lax.rem(b, 2)
        d_pre = dot(dm_t[...], tw2t[...]) * tok_s[slot, 1].astype(F32)
        va[5:6, 0:hidden] += jnp.sum(d_pre, axis=0, keepdims=True)
        d_pre = d_pre.astype(BF)
        tg_a[SPACE:, :] += dot(dm_s[...], tok_s[slot, 0])
        xhat1, rstd1 = standardize(x_in[b].astype(F32), 0)
        n1_s[:, 0:patches] = (xhat1 * cols_s[0, :, 0:1] + cols_s[1, :, 0:1]).astype(BF)
        tg_a[0:SPACE, :] += dot(n1_s[...].T, d_pre)
        dn1 = dot(d_pre, tw1t[...])[:, 0:patches]
        ln1_a[:, 0:1] += jnp.sum(dn1 * xhat1, axis=1, keepdims=True)
        ln1_a[:, 1:2] += jnp.sum(dn1, axis=1, keepdims=True)
        dxh = dn1 * cols_s[0, :, 0:1]
        first = jnp.sum(dxh, axis=0, keepdims=True) / width
        second = jnp.sum(dxh * xhat1, axis=0, keepdims=True) / width
        x_in[b] = (d_mid + rstd1 * (dxh - first - xhat1 * second)).astype(BF)
        for k in range(1, n_mp):
            grad_copy(k, b).start()
        own_grad(b).start()
        for k in range(images):
            if table["image", k]:
                pl.when(b == k)(functools.partial(slot_steps, table["image", k]))
        return 0

    def wait_tokens(b, _):
        for k in range(1, n_mp):
            token_copy(k, b).wait_send()
        return 0

    lax.fori_loop(0, images, wait_tokens, 0)

    for h in range(2):
        wide_load(1, h).wait()
        dn_a[...] = dot_nt(wide_s[:, 0:deep], w1_s[...])
        wide_load(*((1, 1) if h == 0 else (0, 0))).start()
        slot_steps(table["dense", h])
        lax.fori_loop(h * images // 2, (h + 1) * images // 2, token_backward, 0)

    group = groups[0]
    mine = member(group)
    t_half = t_b.shape[0] // 2
    s_rows = t_s2.shape[0]
    w_v = t_b.shape[1]
    va[0:2, :] = ln1_a[...].T[0:2, :]
    for row in range(7):
        for c in range(width // w_v):
            at = ROW + row * 2 + c
            tg_a[at : at + 1, :] = va[row : row + 1, c * w_v : (c + 1) * w_v]
    for c in range(0, deep, 128):
        at, col = ROW + 14 + c // w_v, c % w_v
        tg_a[at : at + 1, col : col + 128] = cb1_a[c // BLOCK, 0:1, c % BLOCK : c % BLOCK + 128]
    t_b[...] = tg_a[...].astype(BF)

    def spot(i):
        return pl.ds(pl.multiple_of(i * s_rows, 16), s_rows)

    def side(i):
        return pl.ds(pl.multiple_of(i * t_half, 16), t_half)

    sem = 0
    core_sum = remote(t_b.at[side(1 - core_bit)], t_r1, sm_s.at[0], sm_r.at[0], partner(core))
    sem += 1
    spread, back = [], []
    for g, team in enumerate(groups):
        copies = []
        for k in range(1, team[1] * team[2]):
            other, to = peer(team, k)
            src = t_r1.at[spot(other)] if g == 0 else t_s2
            copies.append(remote(src, t_r2.at[g, member(team)], sm_s.at[sem], sm_r.at[sem], to))
            sem += 1
        spread.append(copies)
    for k in range(1, group[1] * group[2]):
        _, to = peer(group, k)
        back.append(remote(t_s2, t_g.at[spot(mine)], sm_s.at[sem], sm_r.at[sem], to))
        sem += 1
    t_here = smt_o.at[side(core_bit)]
    core_back = remote(t_g, t_here, sm_s.at[sem], sm_r.at[sem], partner(core))
    own_small = pltpu.make_async_copy(t_g, t_here, sm_l.at[0])

    def sum_team(g):
        count = groups[g][1] * groups[g][2]
        acc = t_r2[g, 0].astype(F32)
        for k in range(1, count):
            acc = acc + t_r2[g, k].astype(F32)
        t_s2[...] = acc.astype(BF)

    core_sum.start()

    def out_rows(h):
        wide_load(0, h).wait()
        result = dot(wide_s[:, 0:deep], w2_s[...])
        for i in range(images // 2):
            b = h * images // 2 + i
            rows = result[i * patches : (i + 1) * patches, :]
            mid_p[b] = (mid_p[b].astype(F32) + rows + rows_s[4:5, :]).astype(BF)
        if h == 0:
            wide_load(0, 1).start()
        slot_steps(table["out", h])

    out_rows(0)
    core_sum.wait()
    t_r1[...] = (t_r1[...].astype(F32) + t_b[side(core_bit), :].astype(F32)).astype(BF)
    start(spread[0])
    t_r2[0, mine] = t_r1[spot(mine), :]
    out_rows(1)
    wait(spread[0])
    sum_team(0)
    for g in range(1, len(groups)):
        start(spread[g])
        t_r2[g, member(groups[g])] = t_s2[...]
        wait(spread[g])
        sum_team(g)
    start(back)
    t_g[spot(mine), :] = t_s2[...]

    for c in range(0, width, 128):
        cols = slice(c, c + 128)
        for b in range(images):
            mix_s[pl.ds(b, patches, stride=images), :] = mid_p[b, :, cols].astype(F32)
        n2_f[:, cols] = mix_s[...].astype(BF)
    own_out = pltpu.make_async_copy(n2_f, out_o, o_l.at[0])
    own_out.start()
    slot_steps(table["end",])
    wait(back)
    core_back.start()
    own_small.start()
    slot_steps(rest_steps)
    core_back.wait()
    own_small.wait()

    def wait_grads(b, _):
        for k in range(1, n_mp):
            other, to = mp_peer(k)
            grad_copy(k, b).wait_send()
            remote(
                x_in.at[b, channels(other)],
                dtok_o.at[other * images + b],
                out_s.at[k - 1, b],
                out_r.at[other, b],
                to,
            ).wait_recv()
        own_grad(b).wait()
        return 0

    lax.fori_loop(0, images, wait_grads, 0)
    own_out.wait()


def finish_kernel(
    out,
    dtok,
    gw,
    smt,
    out_o,
    dtok_o,
    g_ln1,
    b_ln1,
    g_tw1,
    g_tb1,
    g_tw2,
    g_tb2,
    g_ln2,
    b_ln2,
    g_cw1,
    g_cb1,
    g_cw2,
    g_cb2,
):
    @pl.when(pl.program_id(0) == 0)
    def _():
        patches, width = g_tw1.shape[0], g_ln1.shape[0]
        g_tw1[...] = smt[0:patches, :].astype(F32)
        g_tw2[...] = smt[SPACE : SPACE + patches, :].astype(F32)
        per = width // smt.shape[1]
        small = smt[ROW:SPACE, :].astype(F32)
        for row, ref in ((0, g_ln1), (1, b_ln1), (2, g_ln2), (3, b_ln2), (4, g_cb2), (5, g_tb1), (6, g_tb2), (7, g_cb1)):
            n = ref.shape[0]
            rows = [small[row * per + i : row * per + i + 1, :] for i in range(-(-n // smt.shape[1]))]
            ref[...] = jnp.concatenate(rows, axis=1)[:, 0:n].reshape(n)

    g_cw1[...] = gw[0].astype(F32)
    g_cw2[...] = gw[1].astype(F32).T
    out_o[...] = out[...]
    dtok_o[...] = dtok[...]


def body(tokens, cot, g1, c1, tw1, tb1, tw2, tb2, g2, c2, w1, b1, w2, b2):
    n_mp, n_dp = lax.axis_size("mp"), lax.axis_size("dp")
    images, patches, width = cot.shape
    hidden = tw1.shape[1]
    local = tokens.shape[2]
    deep = w1.shape[1]
    tokens = tokens.transpose(0, 2, 1)
    cot = cot.transpose(1, 0, 2).reshape(patches * images, width)
    tw2 = tw2.T
    blocks = deep // BLOCK
    streams = reduce_plan(n_mp, n_dp, width)
    groups = small_groups(n_mp, n_dp)
    total = images * patches
    stage_rows = [have for _, _, stages in streams for _, have, _ in stages]
    n_ids = 1 + len(stage_rows)
    team = groups[0][1] * groups[0][2]
    n_small = 2 + team - 1 + sum(size * across - 1 for _, size, across in groups)
    s_rows = SPACE // team
    hbm, vmem = pl.BlockSpec(memory_space=pl.ANY), pl.BlockSpec(memory_space=pltpu.VMEM)
    dma = pltpu.SemaphoreType.DMA
    scratch = [
        pltpu.VMEM((images, width, patches), BF),
        pltpu.VMEM((patches, width), BF),
        pltpu.VMEM((images, patches, width), BF),
        pltpu.VMEM((total, width), BF),
        pltpu.VMEM((total, width), BF),
        pltpu.VMEM((total // 2, max(deep, 2 * (-(-total // 128) * 128))), BF),
        pltpu.VMEM((2, 2, width, hidden), BF),
        pltpu.VMEM((total // 2, width), F32),
        pltpu.VMEM((patches, width), F32),
        pltpu.VMEM((total, 128), F32),
        pltpu.VMEM((2, 2, total, BLOCK), BF),
        pltpu.VMEM((width, deep), BF),
        pltpu.VMEM((deep, width), BF),
        pltpu.VMEM((2, width, BLOCK), BF),
        pltpu.VMEM((blocks, width, BLOCK), BF),
        [pltpu.VMEM((blocks, rows, BLOCK), BF) for rows in stage_rows],
        pltpu.VMEM((width, SPACE), BF),
        pltpu.VMEM((SPACE, width), BF),
        pltpu.VMEM((width, SPACE), BF),
        pltpu.VMEM((SPACE, hidden), BF),
        pltpu.VMEM((hidden, SPACE), BF),
        pltpu.VMEM((hidden, SPACE), BF),
        pltpu.VMEM((SPACE, hidden), BF),
        pltpu.VMEM((8, width), F32),
        pltpu.VMEM((blocks, 8, BLOCK), F32),
        pltpu.VMEM((2, width, 128), F32),
        pltpu.VMEM((blocks, 8, BLOCK), F32),
        pltpu.VMEM((8, width), F32),
        pltpu.VMEM((width, 128), F32),
        pltpu.VMEM((2 * SPACE, hidden), F32),
        pltpu.VMEM((2 * SPACE, hidden), BF),
        pltpu.VMEM((SPACE, hidden), BF),
        pltpu.VMEM((len(groups), team, s_rows, hidden), BF),
        pltpu.VMEM((s_rows, hidden), BF),
        pltpu.VMEM((SPACE, hidden), BF),
        dma((n_mp - 1, images)),
        dma((n_mp, images)),
        dma((images,)),
        dma((1,)),
        dma((2,)),
        dma((1,)),
        dma((2, 2)),
        dma((2, 2, 2, 2)),
        dma((2, 2)),
        dma((n_mp - 1, images)),
        dma((n_mp, images)),
        dma((images,)),
        dma((n_ids, blocks)),
        dma((n_ids, blocks)),
        dma((n_ids + len(streams), blocks)),
        dma((n_ids + len(streams), blocks)),
        dma((len(streams), blocks)),
        dma((n_small,)),
        dma((n_small,)),
        dma((1,)),
    ]
    out, dtok, gw, smt, _, _ = pl.pallas_call(
        functools.partial(layer_kernel, n_mp, n_dp, streams, groups),
        out_shape=(
            jax.ShapeDtypeStruct(cot.shape, BF),
            jax.ShapeDtypeStruct(tokens.shape, BF),
            jax.ShapeDtypeStruct((2, width, deep), BF),
            jax.ShapeDtypeStruct((2 * SPACE, hidden), BF),
            jax.ShapeDtypeStruct((images, 2, width, hidden), BF),
            jax.ShapeDtypeStruct((2, total, deep), BF),
        ),
        in_specs=[hbm] * 4 + [vmem] * 10,
        out_specs=(hbm,) * 6,
        scratch_shapes=scratch,
        compiler_params=pltpu.CompilerParams(
            collective_id=0, has_side_effects=True, vmem_limit_bytes=VMEM_LIMIT
        ),
    )(tokens, cot, w1, w2, g1, c1, tw1, tb1, tw2, tb2, g2, c2, b1, b2)
    full = lambda n: jax.ShapeDtypeStruct((n,), F32)
    out_spec = pl.BlockSpec((total, width // blocks), lambda j: (0, j))
    dtok_spec = pl.BlockSpec((n_mp * images, local // blocks, patches), lambda j: (0, j, 0))
    results = pl.pallas_call(
        finish_kernel,
        grid=(blocks,),
        out_shape=(
            jax.ShapeDtypeStruct(out.shape, BF),
            jax.ShapeDtypeStruct(dtok.shape, BF),
            full(width),
            full(width),
            jax.ShapeDtypeStruct((patches, hidden), F32),
            full(hidden),
            jax.ShapeDtypeStruct((patches, hidden), F32),
            full(patches),
            full(width),
            full(width),
            jax.ShapeDtypeStruct((width, deep), F32),
            full(deep),
            jax.ShapeDtypeStruct((deep, width), F32),
            full(width),
        ),
        in_specs=[out_spec, dtok_spec, pl.BlockSpec((2, width, BLOCK), lambda j: (0, 0, j)), vmem],
        out_specs=(
            (out_spec, dtok_spec)
            + (vmem,) * 8
            + (
                pl.BlockSpec((width, BLOCK), lambda j: (0, j)),
                vmem,
                pl.BlockSpec((BLOCK, width), lambda j: (j, 0)),
                vmem,
            )
        ),
        compiler_params=pltpu.CompilerParams(vmem_limit_bytes=VMEM_LIMIT),
    )(out, dtok, gw, smt)
    out, dtok, *grads = results
    grads[4] = grads[4].T
    return (out.reshape(patches, images, width).transpose(1, 0, 2), dtok.transpose(0, 2, 1), *grads)


def solution(mesh):
    placed = (P("dp", None, "mp"), P(("dp", "mp"), None, None)) + (P(),) * 12
    return jax.shard_map(body, mesh=mesh, in_specs=placed, out_specs=(placed[1], placed[0]) + (P(),) * 12, check_vma=False)
```

time: 245 us -> 208 us (0.85)
  local copies, waits for them, and re-layouts: 21.2 us -> 0 us
  other arithmetic: 13.7 us -> 0 us
    pallas_call x1, Pallas kernels: 209 us -> 192 us  [body(): pl.pallas_call(functools.partial(layer_kernel, n_mp, n_dp, streams, group...]
    pallas_call x0 -> x1, Pallas kernels: none -> 14.6 us  [body(): pl.pallas_call(finish_kernel, grid=(blocks,), out_shape=(jax.ShapeDtypeSt...]
    unnamed x9 -> x0, local copies, waits for them, and re-layouts: 13.4 us -> none
    convert_element_type x1 -> x0, other arithmetic: 12.8 us -> none  [body(): gw[1].T.astype(F32)]
    slice x10 -> x0, local copies, waits for them, and re-layouts: 7.07 us -> none  [the longest x2 1.46 us: body(): vec[4 * width:5 * width]]
where the time goes in v2:
time: 208 us
  Pallas kernels  207 us (100%)
    pallas_call x1, Pallas kernels, body(): pl.pallas_call(functools.partial(layer_kernel, n_mp, n_dp, streams, group...  192 us
    pallas_call x1, Pallas kernels, body(): pl.pallas_call(finish_kernel, grid=(blocks,), out_shape=(jax.ShapeDtypeSt...  14.6 us

profile of v2, /device:TPU:0, one launch (start us, length us, event | category | flops | bytes accessed | tf_op | source)
XLA Modules:
  0.0 207.7 jit_solution(1132135842639898076)
XLA Ops:
  0.7 192.2 %shard_map.245 = (bf16[1568,768]{1,0:T(8,128)(2,1)}, bf16[32,192,196]{2,1,0:T(8,128)(2,1)}, bf16[2,768,3072]{2,1,0:T(8,128)(2,1)}, bf16[512,384]{1,0:T(8,128)(2,...) custom-call(bf16[32,192,196]{2,1,0:T(8,128)(2,1)} %bitcast.10, bf16[1568,768]{1,0:T(8,128)(2,1)} %bitcast.11, ...), custom_call_target="tpu_custom_call" | custom-call | tf_op jit(solution)/shard_map/pallas_call | solution.py:878
  192.8 14.6 %shard_map.246 = (bf16[1568,768]{1,0:T(8,128)(2,1)}, bf16[32,192,196]{2,1,0:T(8,128)(2,1)}, f32[768]{0:T(1024)}, f32[768]{0:T(1024)}, f32[196,384]{1,0:T(8,128)}...) custom-call(bf16[1568,768]{1,0:T(8,128)(2,1)} %get-tuple-element.32., ...), custom_call_target="tpu_custom_call" | custom-call | tf_op jit(solution)/shard_map/pallas_call | solution.py:898

commit v3 on v2

--- a/solution.py
+++ b/solution.py
@@ -22,29 +22,28 @@
     (),
     (10000,),
     (),
-    (10100, 20000, 30000, 40000),
-    (),
-    (10200, 20001, 30001, 40001, 20100, 40100),
-    (30002, 30100, 20002),
-    (10300, 40002, 20101, 40101, 20200, 30003, 40200, 20003, 30200),
-    (40003, 30101),
-    (10400, 20102, 30102, 40102, 20201, 30201, 40201, 20300, 30300, 20004, 30004, 40004),
-    (20103, 40103, 40300, 30103, 30202),
-    (10500, 20202, 20301, 20400, 30400, 30005, 40104, 40202, 40301, 20005),
-    (20203, 30203, 40203, 20500, 40005, 20104, 30301, 20401, 30104),
-    (40401, 30402, 20403, 20502, 20007, 20106, 20205, 30501, 30106, 40206, 20304, 30304),
-    (20302, 40302, 30302, 30500, 20006, 30105, 40105, 40204),
-    (40303, 20501, 40006, 20204, 30204),
-    (20303, 30303, 40400, 30401, 20402, 30006, 20105, 40106, 40304),
-    (30205, 40205),
-    (40500, 30007, 20008, 40305),
-    (30403, 20503, 30008, 20206, 30206, 30502, 20404),
-    (40402, 40501, 40007, 30107, 20305, 30305, 40306),
-    (30503, 40008, 40107, 30108, 30207, 30404, 20405, 20504),
-    (40403, 40502, 40108, 40207, 30208, 20306, 30306, 20406, 30504, 20505),
-    (40208, 40307, 30405, 20506),
-    (40503, 20107, 30307, 40308, 40404),
-    (30406, 20108, 30308, 30505, 40405, 40504, 30407, 30506, 40406, 30408, 40505, 20207, 30507, 20208, 40407, 40506, 30508, 40408, 40507, 20307, 20407, 20507, 40508, 20308, 20408, 20508),
+    (10100,),
+    (20000, 30000, 40000),
+    (10200,),
+    (30001, 20100, 30100, 40100, 20001),
+    (10300, 40001),
+    (20002, 30002, 20101, 30101, 20200, 40101, 30200, 40200),
+    (10400, 40002, 20300, 30300, 40300),
+    (20003, 30003, 20102, 30102, 40102, 20201, 30201, 40201),
+    (10500, 40003),
+    (20303, 30303, 40303, 20402, 30402, 40402, 30501, 40005, 20006, 40105, 20204, 30204, 20502, 40204, 30105, 20105, 40502),
+    (40103, 20301, 30301, 40301, 30202, 20400, 30400, 40400, 20004),
+    (20103, 30103, 20202, 40202, 20500, 30500, 30004, 40004, 40104, 40500),
+    (30203, 20302, 30302, 40302, 20401, 30401, 40401, 20005),
+    (20203, 40203, 20501, 40501, 30005, 20104, 30104),
+    (30006,),
+    (40403, 20403, 30403, 30502, 40503, 40006, 20503, 30205, 40106, 20205, 20304, 20106, 40205, 30304, 30106, 40304),
+    (20007, 30007),
+    (30503, 20404, 30404, 40404, 20504, 40504),
+    (20008, 30008, 30107, 20206, 30206, 40206, 20305, 30305, 40305),
+    (40007, 20107, 40107, 30108, 20405, 30405, 40405, 30504, 20505, 40505),
+    (40207, 20306, 30306, 40306),
+    (40008, 20108, 40108, 20207, 30207, 40208, 30406, 30505, 20208, 30208, 20406, 40406, 20307, 20506, 40506, 20308, 30506, 40307, 40308, 20407, 20408, 30307, 20507, 30407, 40407, 40507, 30507, 30308, 30408, 20508, 40408, 40508, 30508),
 )
 
 
@@ -104,7 +103,7 @@
 
 
 def plan_steps(blocks, images, streams):
-    pieces = [("block", j, p) for j in range(blocks) for p in range(2)] + [("loop",)] + [("dense", h) for h in range(2)]
+    pieces = [("block", j, p) for j in range(blocks) for p in range(2)] + [("loop",), ("dense",)]
     pieces += [("image", b) for b in range(images)] + [("out", h) for h in range(2)] + [("end",)]
     if len(streams) == 3 and len(PLAN) == len(pieces) + 1:
         return dict(zip(pieces, PLAN)), PLAN[-1]
@@ -313,8 +312,8 @@
 
     aside = -(-total // 128) * 128
 
-    def transpose_rows(src, at):
-        for lo in range(0, total, 128):
+    def transpose_rows(src, at, first=0, last=total):
+        for lo in range(first, last, 128):
             hi = min(lo + 128, total)
             wide_s[0:width, at + lo : at + hi] = src[lo:hi, :].T
 
@@ -356,8 +355,8 @@
         mid_p[b] = dm_t[...].T[0:patches, :]
         return 0
 
-    def second_norm(h):
-        for b in range(h * images // 2, (h + 1) * images // 2):
+    def second_norm(first, last):
+        for b in range(first, last):
             xhat, _ = standardize(mid_p[b].astype(F32), 1)
             n2_f[b * patches : (b + 1) * patches, :] = (xhat * rows_s[2:3, :] + rows_s[3:4, :]).astype(BF)
 
@@ -392,7 +391,7 @@
             copy.wait()
 
     lax.fori_loop(0, images // 2, token_forward, 0)
-    second_norm(0)
+    second_norm(0, images // 2)
     wait(weights)
 
     def early(j, _):
@@ -402,21 +401,29 @@
 
         unit(0, j)
         start(hidden_copies(0, 0, j))
-
-        @pl.when(j < images // 2)
+        cols = pl.ds(pl.multiple_of(j * BLOCK, BLOCK), BLOCK)
+        dn_a[...] += dot_nt(hid_s[lax.rem(j, 2), 1, 0:half, :], w1_s[:, cols])
+
+        @pl.when((j % 2 == 1) & (j < images - 4))
         def _():
-            token_forward(images // 2 + j, 0)
+            token_forward(images // 2 + j // 2, 0)
 
         return 0
 
+    dn_a[...] = jnp.zeros_like(dn_a)
     lax.fori_loop(0, blocks, early, 0)
     for j in range(blocks - 2, blocks):
         wait(hidden_copies(0, 0, j))
     start(hidden_copies(1, 0, 0))
+    lax.fori_loop(images - 2, images - 1, token_forward, 0)
+    second_norm(images // 2, images - 1)
+    ahead = (images - 1) * patches // 128 * 128
+    transpose_rows(n2_f, 0, 0, ahead)
+    lax.fori_loop(images - 1, images, token_forward, 0)
     for b in range(images - 2, images):
         token_save(b).wait()
-    second_norm(1)
-    transpose_rows(n2_f, 0)
+    second_norm(images - 1, images)
+    transpose_rows(n2_f, 0, ahead)
 
     core = ("mp", 0)
     core_bit = bit_of(core)
@@ -462,7 +469,7 @@
         def step(i, _):
             here = pl.ds(pl.multiple_of(i * chunk, 16), chunk)
             there = pl.ds(pl.multiple_of(low + i * chunk, 16), chunk)
-            result = (dst[here, :].astype(F32) + src[there, :].astype(F32)).astype(BF)
+            result = dst[here, :] + src[there, :]
             if into is None:
                 dst[here, :] = result
             else:
@@ -574,7 +581,7 @@
     def wide_load(i, h):
         return pltpu.make_async_copy(hid_h.at[i, pl.ds(h * half, half)], wide_s.at[:, pl.ds(0, deep)], wide_l.at[i, h])
 
-    wide_load(1, 0).start()
+    wide_load(1, 1).start()
     token_load(0).start()
 
     def grad_copy(k, b):
@@ -644,10 +651,11 @@
     lax.fori_loop(0, images, wait_tokens, 0)
 
     for h in range(2):
-        wide_load(1, h).wait()
-        dn_a[...] = dot_nt(wide_s[:, 0:deep], w1_s[...])
-        wide_load(*((1, 1) if h == 0 else (0, 0))).start()
-        slot_steps(table["dense", h])
+        if h == 1:
+            wide_load(1, 1).wait()
+            dn_a[...] = dot_nt(wide_s[:, 0:deep], w1_s[...])
+            wide_load(0, 0).start()
+            slot_steps(table["dense",])
         lax.fori_loop(h * images // 2, (h + 1) * images // 2, token_backward, 0)
 
     group = groups[0]
@@ -893,11 +901,11 @@
         ),
     )(tokens, cot, w1, w2, g1, c1, tw1, tb1, tw2, tb2, g2, c2, b1, b2)
     full = lambda n: jax.ShapeDtypeStruct((n,), F32)
-    out_spec = pl.BlockSpec((total, width // blocks), lambda j: (0, j))
-    dtok_spec = pl.BlockSpec((n_mp * images, local // blocks, patches), lambda j: (0, j, 0))
+    out_spec = pl.BlockSpec((total, width // blocks), lambda j: (0, j // 2))
+    dtok_spec = pl.BlockSpec((n_mp * images // 2, local // blocks, patches), lambda j: (j % 2, j // 2, 0))
     results = pl.pallas_call(
         finish_kernel,
-        grid=(blocks,),
+        grid=(2 * blocks,),
         out_shape=(
             jax.ShapeDtypeStruct(out.shape, BF),
             jax.ShapeDtypeStruct(dtok.shape, BF),
@@ -914,14 +922,14 @@
             jax.ShapeDtypeStruct((deep, width), F32),
             full(width),
         ),
-        in_specs=[out_spec, dtok_spec, pl.BlockSpec((2, width, BLOCK), lambda j: (0, 0, j)), vmem],
+        in_specs=[out_spec, dtok_spec, pl.BlockSpec((2, width, BLOCK // 2), lambda j: (0, 0, j)), vmem],
         out_specs=(
             (out_spec, dtok_spec)
             + (vmem,) * 8
             + (
-                pl.BlockSpec((width, BLOCK), lambda j: (0, j)),
+                pl.BlockSpec((width, BLOCK // 2), lambda j: (0, j)),
                 vmem,
-                pl.BlockSpec((BLOCK, width), lambda j: (j, 0)),
+                pl.BlockSpec((BLOCK // 2, width), lambda j: (j, 0)),
                 vmem,
             )
         ),

time: 208 us -> 191 us (0.918)
  Pallas kernels: 207 us -> 189 us
    pallas_call x1, Pallas kernels: 192 us -> 171 us  [body(): pl.pallas_call(functools.partial(layer_kernel, n_mp, n_dp, streams, group...]
    pallas_call x1, Pallas kernels: 14.6 us -> 18.4 us  [body(): pl.pallas_call(finish_kernel, grid=(2 * blocks,), out_shape=(jax.ShapeDty...]
where the time goes in v3:
time: 191 us; the launch traced here: 190 us
  Pallas kernels  189 us (99%)
    pallas_call x1, Pallas kernels, body(): pl.pallas_call(functools.partial(layer_kernel, n_mp, n_dp, streams, group...  171 us
    pallas_call x1, Pallas kernels, body(): pl.pallas_call(finish_kernel, grid=(2 * blocks,), out_shape=(jax.ShapeDty...  18.4 us

profile of v3, /device:TPU:0, one launch (start us, length us, event | category | flops | bytes accessed | tf_op | source)
XLA Modules:
  0.0 190.3 jit_solution(16103929519036676672)
XLA Ops:
  0.7 171.1 %shard_map.245 = (bf16[1568,768]{1,0:T(8,128)(2,1)}, bf16[32,192,196]{2,1,0:T(8,128)(2,1)}, bf16[2,768,3072]{2,1,0:T(8,128)(2,1)}, bf16[512,384]{1,0:T(8,128)(2,...) custom-call(bf16[32,192,196]{2,1,0:T(8,128)(2,1)} %bitcast.10, bf16[1568,768]{1,0:T(8,128)(2,1)} %bitcast.11, ...), custom_call_target="tpu_custom_call" | custom-call | tf_op jit(solution)/shard_map/pallas_call | solution.py:886
  171.7 18.4 %shard_map.246 = (bf16[1568,768]{1,0:T(8,128)(2,1)}, bf16[32,192,196]{2,1,0:T(8,128)(2,1)}, f32[768]{0:T(1024)}, f32[768]{0:T(1024)}, f32[196,384]{1,0:T(8,128)}...) custom-call(bf16[1568,768]{1,0:T(8,128)(2,1)} %get-tuple-element.32., ...), custom_call_target="tpu_custom_call" | custom-call | tf_op jit(solution)/shard_map/pallas_call | solution.py:906

commit v4 on v3

--- a/solution.py
+++ b/solution.py
@@ -204,33 +204,35 @@
     mp_me = lax.axis_index("mp")
     dp_me = lax.axis_index("dp")
 
-    def bit_of(key):
+    bits, partners = {}, {}
+    for key in [("mp", b) for b in range(bits_of(n_mp))] + [("dp", b) for b in range(bits_of(n_dp))]:
         axis, b = key
         me = mp_me if axis == "mp" else dp_me
-        return (me // (1 << b)) % 2
-
-    def partner(key):
-        axis, b = key
-        me = mp_me if axis == "mp" else dp_me
-        return {axis: me + (1 << b) * (1 - 2 * bit_of(key))}
-
-    def member(group):
+        bits[key] = lax.rem(lax.div(me, 1 << b), 2)
+        partners[key] = {axis: me + (1 << b) * (1 - 2 * bits[key])}
+    bit_of, partner = bits.__getitem__, partners.__getitem__
+
+    members, peers = {}, {}
+    for group in groups:
         stride, size, across = group
-        index = (dp_me // stride) % size
-        return index * across + mp_me // 2 if across > 1 else index
+        index = lax.rem(lax.div(dp_me, stride), size)
+        members[group] = index * across + lax.div(mp_me, 2) if across > 1 else index
+        peers[group] = []
+        for k in range(1, size * across):
+            other = lax.rem(members[group] + k, size * across)
+            to = {"dp": dp_me + (lax.div(other, across) - index) * stride}
+            if across > 1:
+                to["mp"] = lax.rem(other, across) * 2 + lax.rem(mp_me, 2)
+            peers[group].append((other, to))
+    member = members.__getitem__
 
     def peer(group, k):
-        stride, size, across = group
-        mine = member(group)
-        other = lax.rem(mine + k, size * across)
-        to = {"dp": dp_me + (other // across - (dp_me // stride) % size) * stride}
-        if across > 1:
-            to["mp"] = (other % across) * 2 + mp_me % 2
-        return other, to
+        return peers[group][k - 1]
+
+    mp_peers = [lax.rem(mp_me + k, n_mp) for k in range(n_mp)]
 
     def mp_peer(k):
-        other = lax.rem(mp_me + k, n_mp)
-        return other, {"mp": other}
+        return mp_peers[k], {"mp": mp_peers[k]}
 
     def remote(src, dst, send, recv, to):
         return pltpu.make_async_remote_copy(
@@ -901,11 +903,11 @@
         ),
     )(tokens, cot, w1, w2, g1, c1, tw1, tb1, tw2, tb2, g2, c2, b1, b2)
     full = lambda n: jax.ShapeDtypeStruct((n,), F32)
-    out_spec = pl.BlockSpec((total, width // blocks), lambda j: (0, j // 2))
-    dtok_spec = pl.BlockSpec((n_mp * images // 2, local // blocks, patches), lambda j: (j % 2, j // 2, 0))
+    out_spec = pl.BlockSpec((total, width // blocks), lambda j: (0, j))
+    dtok_spec = pl.BlockSpec((n_mp * images, local // blocks, patches), lambda j: (0, j, 0))
     results = pl.pallas_call(
         finish_kernel,
-        grid=(2 * blocks,),
+        grid=(blocks,),
         out_shape=(
             jax.ShapeDtypeStruct(out.shape, BF),
             jax.ShapeDtypeStruct(dtok.shape, BF),
@@ -922,14 +924,14 @@
             jax.ShapeDtypeStruct((deep, width), F32),
             full(width),
         ),
-        in_specs=[out_spec, dtok_spec, pl.BlockSpec((2, width, BLOCK // 2), lambda j: (0, 0, j)), vmem],
+        in_specs=[out_spec, dtok_spec, pl.BlockSpec((2, width, BLOCK), lambda j: (0, 0, j)), vmem],
         out_specs=(
             (out_spec, dtok_spec)
             + (vmem,) * 8
             + (
-                pl.BlockSpec((width, BLOCK // 2), lambda j: (0, j)),
+                pl.BlockSpec((width, BLOCK), lambda j: (0, j)),
                 vmem,
-                pl.BlockSpec((BLOCK // 2, width), lambda j: (j, 0)),
+                pl.BlockSpec((BLOCK, width), lambda j: (j, 0)),
                 vmem,
             )
         ),

time: 191 us -> 187 us (0.979)
  Pallas kernels: 189 us -> 186 us
    pallas_call x1, Pallas kernels: 18.4 us -> 14.6 us  [body(): pl.pallas_call(finish_kernel, grid=(blocks,), out_shape=(jax.ShapeDtypeSt...]
where the time goes in v4:
time: 187 us
  Pallas kernels  186 us (99%)
    pallas_call x1, Pallas kernels, body(): pl.pallas_call(functools.partial(layer_kernel, n_mp, n_dp, streams, group...  171 us
    pallas_call x1, Pallas kernels, body(): pl.pallas_call(finish_kernel, grid=(blocks,), out_shape=(jax.ShapeDtypeSt...  14.6 us

profile of v4, /device:TPU:0, one launch (start us, length us, event | category | flops | bytes accessed | tf_op | source)
XLA Modules:
  0.0 186.6 jit_solution(5250482332303175445)
XLA Ops:
  0.7 171.1 %shard_map.245 = (bf16[1568,768]{1,0:T(8,128)(2,1)}, bf16[32,192,196]{2,1,0:T(8,128)(2,1)}, bf16[2,768,3072]{2,1,0:T(8,128)(2,1)}, bf16[512,384]{1,0:T(8,128)(2,...) custom-call(bf16[32,192,196]{2,1,0:T(8,128)(2,1)} %bitcast.10, bf16[1568,768]{1,0:T(8,128)(2,1)} %bitcast.11, ...), custom_call_target="tpu_custom_call" | custom-call | tf_op jit(solution)/shard_map/pallas_call | solution.py:888
  171.7 14.6 %shard_map.246 = (bf16[1568,768]{1,0:T(8,128)(2,1)}, bf16[32,192,196]{2,1,0:T(8,128)(2,1)}, f32[768]{0:T(1024)}, f32[768]{0:T(1024)}, f32[196,384]{1,0:T(8,128)}...) custom-call(bf16[1568,768]{1,0:T(8,128)(2,1)} %get-tuple-element.32., ...), custom_call_target="tpu_custom_call" | custom-call | tf_op jit(solution)/shard_map/pallas_call | solution.py:908
